TPU v7x, 128 devices: a whole 4x4x4 slice. The times are simulated.
128 devices in a mesh: ctx: 16 (over z, y), hg: 8 (over x, core).
Axes of the slice: x: 4, y: 4, z: 4, core: 2. Of those that a mesh axis runs over, the one named last changes fastest.
Arguments:
- queries: bfloat16 [2, 16, 8192, 256], P(None, None, ('ctx', 'hg')), may hold values from -6 to 6
- keys: bfloat16 [2, 16, 8192, 256], P(None, None, ('ctx', 'hg')), may hold values from -6 to 6
- values: bfloat16 [2, 16, 8192, 256], P(None, None, ('ctx', 'hg')), may hold values from -6 to 6
- rates: bfloat16 [2, 16, 8192], P(None, None, ('ctx', 'hg')), may hold values from 0.099609375 to 1
- step_sizes: float32 [16], P('hg'), may hold values from 0.3 to 1.5
- w_gate: float32 [16, 256, 1024], P('hg'), may hold values from -0.375 to 0.375
- w_up: float32 [16, 256, 1024], P('hg'), may hold values from -0.375 to 0.375
- w_down: float32 [16, 256, 1024], P('hg'), may hold values from -0.1875 to 0.1875
Outputs:
- outputs: float32 [2, 16, 8192, 256], P(None, None, ('ctx', 'hg'))
- gate_final: float32 [16, 256, 1024], P('hg')
- up_final: float32 [16, 256, 1024], P('hg')
- down_final: float32 [16, 256, 1024], P('hg')
All inputs are finite; a program needn't handle non-finite values.
Results may differ from a plain program's by a relative error of at most 0.039.
Values may be sent and summed in bfloat16 or wider, within the bound.
No kernel may reach another device: no remote copies, remote signals or barrier semaphores. Data moves between devices by JAX's collectives and lax.ppermute only.
A program may use at most 128 MiB of HBM per device.

v0:
```python
import jax
import jax.numpy as jnp
from jax import lax
from jax.sharding import PartitionSpec as P

GROUPS = 2
NS_STEPS = 5


coef_a = 3.4445
coef_b = -4.775
coef_c = 2.0315


def ortho_start(grads, total):
    rounded = grads.astype(jnp.bfloat16).astype(jnp.float32)
    return (rounded / (jnp.sqrt(total)[:, :, None, None] + 1e-07)).astype(jnp.bfloat16)


def squares(grads):
    rounded = grads.astype(jnp.bfloat16).astype(jnp.float32)
    return jnp.sum(rounded * rounded, axis=(2, 3))


def poly_step(ortho, gram_sum):
    gram = gram_sum.astype(jnp.bfloat16)
    square = jnp.einsum("mhde,mhef->mhdf", gram, gram, preferred_element_type=jnp.float32)
    poly = (coef_b * gram.astype(jnp.float32) + coef_c * square).astype(jnp.bfloat16)
    moved = jnp.einsum("mhde,mhef->mhdf", poly, ortho, preferred_element_type=jnp.float32)
    return (coef_a * ortho.astype(jnp.float32) + moved).astype(jnp.bfloat16)


def self_gram(ortho):
    return jnp.einsum("mhdf,mhef->mhde", ortho, ortho, preferred_element_type=jnp.float32)


def orthogonal_update(stacked):
    whole = lax.psum(stacked, "ctx")
    ortho = ortho_start(whole, squares(whole))
    for step in range(NS_STEPS):
        ortho = poly_step(ortho, self_gram(ortho))
    return ortho


def shards(queries, keys, values, rates, step_sizes, w_gate, w_up, w_down):
    queries, keys, values, rates = (
        lax.all_to_all(queries, "hg", split_axis=1, concat_axis=2, tiled=True),
        lax.all_to_all(keys, "hg", split_axis=1, concat_axis=2, tiled=True),
        lax.all_to_all(values, "hg", split_axis=1, concat_axis=2, tiled=True),
        lax.all_to_all(rates, "hg", split_axis=1, concat_axis=2, tiled=True),
    )
    weights = jnp.stack([w_gate, w_up, w_down])
    outs = []
    for group in range(GROUPS):
        bweights = weights.astype(jnp.bfloat16)
        key_c = keys[group]
        gate = jnp.einsum("htd,hdf->htf", key_c, bweights[0], preferred_element_type=jnp.float32)
        upval = jnp.einsum("htd,hdf->htf", key_c, bweights[1], preferred_element_type=jnp.float32)
        active = jax.nn.silu(gate)
        hidden = (active * upval).astype(jnp.bfloat16)
        dout = (
            -rates[group].astype(jnp.float32)[:, :, None] * values[group].astype(jnp.float32)
        ).astype(jnp.bfloat16)
        grad_down = jnp.einsum("htd,htf->hdf", dout, hidden, preferred_element_type=jnp.float32)
        dhid = jnp.einsum("htd,hdf->htf", dout, bweights[2], preferred_element_type=jnp.float32)
        sigma = jax.nn.sigmoid(gate)
        d_gate = (dhid * upval * sigma * (1.0 + gate * (1.0 - sigma))).astype(jnp.bfloat16)
        d_up = (dhid * active).astype(jnp.bfloat16)
        grad_gate = jnp.einsum("htd,htf->hdf", key_c, d_gate, preferred_element_type=jnp.float32)
        grad_up = jnp.einsum("htd,htf->hdf", key_c, d_up, preferred_element_type=jnp.float32)
        ortho = orthogonal_update(jnp.stack([grad_gate, grad_up, grad_down]))
        cand = weights - step_sizes[None, :, None, None] * ortho.astype(jnp.float32)
        scale = jnp.sqrt(jnp.sum(weights * weights, axis=2, keepdims=True) + 1e-06) / jnp.sqrt(
            jnp.sum(cand * cand, axis=2, keepdims=True) + 1e-06
        )
        weights = cand * scale
        bweights = weights.astype(jnp.bfloat16)
        query_c = queries[group]
        q_gate = jnp.einsum(
            "htd,hdf->htf", query_c, bweights[0], preferred_element_type=jnp.float32
        )
        q_up = jnp.einsum("htd,hdf->htf", query_c, bweights[1], preferred_element_type=jnp.float32)
        q_hid = (jax.nn.silu(q_gate) * q_up).astype(jnp.bfloat16)
        result = jnp.einsum("htf,hdf->htd", q_hid, bweights[2], preferred_element_type=jnp.float32)
        outs.append(result)
    gathered = lax.all_to_all(jnp.stack(outs), "hg", split_axis=2, concat_axis=1, tiled=True)
    return (gathered, weights[0], weights[1], weights[2])


def solution(mesh):
    return jax.shard_map(
        shards,
        mesh=mesh,
        in_specs=(
            P(None, None, ("ctx", "hg"), None),
            P(None, None, ("ctx", "hg"), None),
            P(None, None, ("ctx", "hg"), None),
            P(None, None, ("ctx", "hg")),
            P("hg"),
            P("hg", None, None),
            P("hg", None, None),
            P("hg", None, None),
        ),
        out_specs=(
            P(None, None, ("ctx", "hg"), None),
            P("hg", None, None),
            P("hg", None, None),
            P("hg", None, None),
        ),
        check_vma=False,
    )
```

profile of v0, /device:TPU:1, one launch (start us, length us, event | category | flops | bytes accessed | tf_op | source)
XLA Modules:
  0.0 548.4 jit_solution(237282445799500552)
XLA Ops:
  2.1 5.8 %all-to-all-start = ((bf16[8,2,128]{2,1,0:T(2,128)(2,1)}), bf16[8,2,128]{2,1,0:T(2,128)(2,1)S(1)}, u32[]{:S(2)}, u32[]{:S(2)}) async-start(bf16[8,2,128]{2,1,0:T(2,128)(2,1)} %reshape.87), calls=%async_computation | async-start | bytes 8192 | tf_op jit(solution)/shard_map/all_to_all | solution.py:50
  25.0 7.4 %all-to-all-done.2 = bf16[2,16,64,256]{3,2,0,1:T(8,128)(2,1)} async-done(((bf16[2,16,64,256]{3,2,0,1:T(8,128)(2,1)}), bf16[2,16,64,256]{3,2,0,1:T(8,128)(2,1)}, u32[]{:S(2)}, u32[]{:S(2)}) %all-to-all-start.2) | async-done | bytes 1048608 | tf_op jit(solution)/shard_map/all_to_all | solution.py:48
  32.5 5.0 all-to-all-start.1
  45.0 7.7 %all-to-all-done.1 = bf16[2,16,64,256]{3,2,0,1:T(8,128)(2,1)} async-done(((bf16[2,16,64,256]{3,2,0,1:T(8,128)(2,1)}), bf16[2,16,64,256]{3,2,0,1:T(8,128)(2,1)}, u32[]{:S(2)}, u32[]{:S(2)}) %all-to-all-start.1) | async-done | bytes 1048608 | tf_op jit(solution)/shard_map/all_to_all | solution.py:49
  52.7 5.0 all-to-all-start.3
  72.2 145.8 %all-reduce.2 = bf16[3,2,256,1024]{3,2,1,0:T(8,128)(2,1)S(1)} all-reduce(f32[3,2,256,1024]{3,2,1,0:T(8,128)} %pad_maximum_fusion.1), channel_id=1, replica_groups=mesh['ctx'=16,'hg'=8] {'ctx'}, use_global_device_ids=true, to_apply=%region_0.1 | all-reduce | flops 1572864 | bytes 9437184 | tf_op jit(solution)/shard_map/psum | solution.py:38
  223.6 4.9 add_convert_fusion.9
  235.2 4.9 convolution_convert_fusion.7
  244.9 4.9 convolution_convert_fusion.6
  258.7 7.9 %multiply_reduce_fusion.2 = (f32[3,2,1024]{2,1,0:T(2,128)S(1)}, f32[3,2,256,1024]{3,2,1,0:T(8,128)}) fusion(bf16[3,2,256,1024]{3,2,1,0:T(8,128)(2,1)} %add_convert_fusion.6, bf16[3,2,256,256]{3,2,1,0:T(8,128)(2,1)S(1)} %convolution_convert_fusion.5, f32[2]{0:T(128)S(1)} %copy-done.16, f32[1,2,256,1024]{3,2,1,0:T(8,128)S(1)} %bitcast.294, ...), kind=kOutput, calls=%fused_computation.19 | convolution fusion | flops 1025894400 | bytes 16539656 | tf_op jit(solution)/shard_map/mhde,mhef->mhdf/dot_general | solution.py:29
  288.0 5.1 convolution_bitcast_fusion.1
  293.1 6.6 %pad_maximum_fusion.2 = f32[3,2,256,1024]{3,2,1,0:T(8,128)} fusion(f32[1,2,256,1024]{3,2,1,0:T(8,128)} %fusion.40, f32[1,2,256,1024]{3,2,1,0:T(8,128)} %fusion.46, f32[1,2,256,1024]{3,2,1,0:T(8,128)} %fusion.48), kind=kLoop, calls=%fused_computation.10 | loop fusion | flops 3145728 | bytes 12582912 | tf_op jit(solution)/shard_map/stack | solution.py:71
  299.7 136.1 %all-reduce.3 = bf16[3,2,256,1024]{3,2,1,0:T(8,128)(2,1)S(1)} all-reduce(f32[3,2,256,1024]{3,2,1,0:T(8,128)} %pad_maximum_fusion.2), channel_id=1, replica_groups=mesh['ctx'=16,'hg'=8] {'ctx'}, use_global_device_ids=true, to_apply=%region_4.5 | all-reduce | flops 1572864 | bytes 9437184 | tf_op jit(solution)/shard_map/psum | solution.py:38
  441.5 5.0 add_convert_fusion.4
  448.4 4.9 add_convert_fusion.3
  453.4 4.9 convolution_convert_fusion.2
  458.3 4.9 add_convert_fusion.2
  467.9 5.0 add_convert_fusion.1
  476.5 10.2 %multiply_reduce_fusion.1 = (f32[3,2,1024]{2,1,0:T(2,128)S(1)}, f32[3,2,1024]{2,1,0:T(2,128)S(1)}, bf16[3,2,256,1024]{3,2,1,0:T(8,128)(2,1)}) fusion(f32[3,2,256,1024]{3,2,1,0:T(8,128)} %get-tuple-element.20, f32[3,2,1024]{2,1,0:T(2,128)S(1)} %rsqrt_multiply_fusion.1, f32[2]{0:T(128)S(1)} %copy-done.16, bf16[3,2,256,1024]{3,2,1,0:T(8,128)(2,1)} %copy-done.17, ...), kind=kOutput, calls=%fused_computation.12 | convolution fusion | flops 1027461120 | bytes 13443080 | tf_op jit(solution)/shard_map/mhde,mhef->mhdf/dot_general | solution.py:29
  486.8 8.3 %fusion.110 = (bf16[3,2,256,1024]{3,2,1,0:T(8,128)(2,1)S(1)}, f32[3,2,256,1024]{3,2,1,0:T(8,128)}) fusion(f32[3,2,1024]{2,1,0:T(2,128)S(1)} %rsqrt_multiply_fusion, bf16[3,2,256,1024]{3,2,1,0:T(8,128)(2,1)} %get-tuple-element.21, f32[2]{0:T(128)S(1)} %copy-done.16, f32[3,2,256,1024]{3,2,1,0:T(8,128)} %get-tuple-element.20, ...), kind=kLoop, calls=%fused_computation.188 | loop fusion | flops 9437184 | bytes 18923528 | tf_op jit(solution)/shard_map/convert_element_type | solution.py:77
  497.8 5.1 convolution_bitcast_fusion
  507.5 12.7 %all-to-all-start.4 = ((f32[2,2,512,256]{3,1,0,2:T(2,128)}), f32[2,2,512,256]{3,1,0,2:T(2,128)S(1)}, u32[]{:S(2)}, u32[]{:S(2)}) async-start(f32[2,2,512,256]{3,1,0,2:T(2,128)} %copy.133), calls=%async_computation.4 | async-start | bytes 4194304 | tf_op jit(solution)/shard_map/all_to_all | solution.py:86
  520.2 5.8 %slice_bitcast_fusion = (f32[2,256,1024]{2,1,0:T(8,128)}, f32[2,256,1024]{2,1,0:T(8,128)}, f32[2,256,1024]{2,1,0:T(8,128)}) fusion(f32[3,2,256,1024]{3,2,1,0:T(8,128)} %get-tuple-element.7), kind=kLoop, calls=%fused_computation.76 | loop fusion | bytes 12582912 | tf_op jit(solution)/shard_map/squeeze | solution.py:87
  526.0 20.5 %all-to-all-done.4 = f32[2,2,512,256]{3,1,0,2:T(2,128)S(1)} async-done(((f32[2,2,512,256]{3,1,0,2:T(2,128)}), f32[2,2,512,256]{3,1,0,2:T(2,128)S(1)}, u32[]{:S(2)}, u32[]{:S(2)}) %all-to-all-start.4) | async-done | bytes 2097184 | tf_op jit(solution)/shard_map/all_to_all | solution.py:86
  (102 shorter events, 112.9 us)
Async XLA Ops:
  0.6 16.6 %copy-start.14 = (bf16[2,16,64,256]{3,2,1,0:T(8,128)(2,1)S(1)}, bf16[2,16,64,256]{3,2,1,0:T(8,128)(2,1)}, u32[]{:S(2)}) copy-start(bf16[2,16,64,256]{3,2,1,0:T(8,128)(2,1)} %param.10) | copy-start | bytes 3145732
  2.1 10.3 %all-to-all-start = ((bf16[8,2,128]{2,1,0:T(2,128)(2,1)}), bf16[8,2,128]{2,1,0:T(2,128)(2,1)S(1)}, u32[]{:S(2)}, u32[]{:S(2)}) async-start(bf16[8,2,128]{2,1,0:T(2,128)(2,1)} %reshape.87), calls=%async_computation | async-start | bytes 8192 | tf_op jit(solution)/shard_map/all_to_all | solution.py:50
  7.9 10.4 %copy-start.15 = (bf16[2,16,64,256]{3,2,1,0:T(8,128)(2,1)S(1)}, bf16[2,16,64,256]{3,2,1,0:T(8,128)(2,1)}, u32[]{:S(2)}) copy-start(bf16[2,16,64,256]{3,2,1,0:T(8,128)(2,1)} %param.8) | copy-start | bytes 3145732
  12.4 20.0 %all-to-all-start.2 = ((bf16[2,16,64,256]{3,2,0,1:T(8,128)(2,1)}), bf16[2,16,64,256]{3,2,0,1:T(8,128)(2,1)}, u32[]{:S(2)}, u32[]{:S(2)}) async-start(bf16[2,16,64,256]{3,2,0,1:T(8,128)(2,1)} %copy.102), calls=%async_computation.2 | async-start | bytes 2097152 | tf_op jit(solution)/shard_map/all_to_all | solution.py:48
  19.3 3.6 copy-start
  19.3 4.1 copy-start.2
  19.3 4.7 copy-start.3
  32.5 20.2 %all-to-all-start.1 = ((bf16[2,16,64,256]{3,2,0,1:T(8,128)(2,1)}), bf16[2,16,64,256]{3,2,0,1:T(8,128)(2,1)}, u32[]{:S(2)}, u32[]{:S(2)}) async-start(bf16[2,16,64,256]{3,2,0,1:T(8,128)(2,1)} %copy.99), calls=%async_computation.1 | async-start | bytes 2097152 | tf_op jit(solution)/shard_map/all_to_all | solution.py:49
  39.6 2.7 copy-start.5
  52.7 229.6 %all-to-all-start.3 = ((bf16[2,16,64,256]{3,2,0,1:T(8,128)(2,1)}), bf16[2,16,64,256]{3,2,0,1:T(8,128)(2,1)}, u32[]{:S(2)}, u32[]{:S(2)}) async-start(bf16[2,16,64,256]{3,2,0,1:T(8,128)(2,1)} %copy.113), calls=%async_computation.3 | async-start | bytes 2097152 | tf_op jit(solution)/shard_map/all_to_all | solution.py:47
  60.3 2.3 copy-start.8
  62.6 2.2 copy-start.9
  220.1 1.6 copy-start.10
  235.2 4.9 copy-start.18
  244.9 4.9 copy-start.19
  254.7 4.0 copy-start.1
  254.7 4.0 copy-start.16
  266.6 3.8 copy-start.4
  271.1 1.2 copy-start.7
  437.9 1.7 copy-start.11
  453.4 4.9 copy-start.20
  472.9 1.7 copy-start.17
  486.8 8.3 %copy-start.12 = (bf16[1,2,8,64,256]{4,3,2,1,0:T(8,128)(2,1)S(1)}, bf16[1,2,8,64,256]{4,3,2,1,0:T(8,128)(2,1)}, u32[]{:S(2)}) copy-start(bf16[1,2,8,64,256]{4,3,2,1,0:T(8,128)(2,1)} %get-tuple-element.12) | copy-start | bytes 1572868
  507.5 39.0 %all-to-all-start.4 = ((f32[2,2,512,256]{3,1,0,2:T(2,128)}), f32[2,2,512,256]{3,1,0,2:T(2,128)S(1)}, u32[]{:S(2)}, u32[]{:S(2)}) async-start(f32[2,2,512,256]{3,1,0,2:T(2,128)} %copy.133), calls=%async_computation.4 | async-start | bytes 4194304 | tf_op jit(solution)/shard_map/all_to_all | solution.py:86
  (2 other events, 1.8 us)
where the time goes:
time: 556 us; the launch traced here: 548 us
  blocking collectives  282 us (51%)
  matrix products  129 us (23%)
  waiting for transfers between devices  37.8 us (7%)
  other arithmetic  33.6 us (6%)
  starting transfers between devices  33.3 us (6%)
  local copies, waits for them, and re-layouts  32.2 us (6%)
    psum x2, blocking collectives, orthogonal_update(): whole = lax.psum(stacked, 'ctx')  282 us
    dot_general x10, matrix products, poly_step(): jnp.einsum('mhde,mhef->mhdf', poly, ortho, preferred_element_type=jnp.flo...  57.3 us
    dot_general x10, matrix products, self_gram(): jnp.einsum('mhdf,mhef->mhde', ortho, ortho, preferred_element_type=jnp.fl...  32.8 us
    all_to_all x1, waiting for transfers between devices, shards(): lax.all_to_all(jnp.stack(outs), 'hg', split_axis=2, concat_axis=1, tiled=...  20.5 us
    unnamed x48, local copies, waits for them, and re-layouts  15.7 us
    convert_element_type x3, other arithmetic, shards(): bweights = weights.astype(jnp.bfloat16)  15.7 us
    all_to_all x1, starting transfers between devices, shards(): lax.all_to_all(jnp.stack(outs), 'hg', split_axis=2, concat_axis=1, tiled=...  12.7 us
  transfers between devices with their start and end apart: 5, of which 4 were waited for; matrix products, arithmetic and copies ran while one was open for 18% of the time, Pallas kernels for 0%

commit v1 on v0

v1 whole, which is shorter than its diff:
```python
import functools

import jax
import jax.numpy as jnp
from jax import lax
from jax.experimental import pallas as pl
from jax.experimental.pallas import tpu as pltpu
from jax.sharding import Mesh
from jax.sharding import PartitionSpec as P

GROUPS = 2
NS_STEPS = 5
DH = 256
FF = 1024
HALF = FF // 2
LANE = 128
TOK = 1024
TILE = 512

coef_a = 3.4445
coef_b = -4.775
coef_c = 2.0315

f32 = jnp.float32
bf16 = jnp.bfloat16
MIB = 1024 * 1024

VSPEC = pl.BlockSpec(memory_space=pltpu.VMEM)
ANYSPEC = pl.BlockSpec(memory_space=pl.ANY)
HBMSPEC = pl.BlockSpec(memory_space=pltpu.HBM)
SSPEC = pl.BlockSpec(memory_space=pltpu.SMEM)


def dot(a, b, dims):
    return lax.dot_general(a, b, (dims, ((), ())), preferred_element_type=f32)


def params(mib):
    return pltpu.CompilerParams(vmem_limit_bytes=mib * MIB)


def cost(flops, size, transcendentals=0):
    return pl.CostEstimate(flops=flops, bytes_accessed=size, transcendentals=transcendentals)


def after(value, *earlier):
    return lax.optimization_barrier((value, earlier))[0]


def pack_kernel(key_ref, value_ref, rate_ref, *out_refs):
    for group, out_ref in enumerate(out_refs):
        out_ref[:, :, :DH] = key_ref[group]
        rate = -rate_ref[group].astype(f32)
        out_ref[:, :, DH:] = (rate[:, :, None] * value_ref[group].astype(f32)).astype(bf16)


def pack(keys, values, rates):
    heads = 8
    spec = pl.BlockSpec((GROUPS, heads, 64, DH), lambda i: (0, i, 0, 0))
    return pl.pallas_call(
        pack_kernel,
        grid=(16 // heads,),
        out_shape=[jax.ShapeDtypeStruct((16, 64, 2 * DH), bf16)] * GROUPS,
        in_specs=[spec, spec, pl.BlockSpec((GROUPS, heads, 64), lambda i: (0, i, 0))],
        out_specs=[pl.BlockSpec((heads, 64, 2 * DH), lambda i: (i, 0, 0))] * GROUPS,
        compiler_params=params(56),
        name="pack",
        cost_estimate=cost(1, 1),
    )(keys, values, rates)


def join_kernel(own_ref, peer_ref, queries_ref, *refs):
    out_ref = refs[-1]
    out_ref[:, :, : 2 * DH] = own_ref[...]
    out_ref[:, :, 2 * DH : 4 * DH] = peer_ref[...]
    for group in range(GROUPS):
        out_ref[:, :, (4 + group) * DH : (5 + group) * DH] = queries_ref[group]


def join(own, peer, queries, *earlier):
    heads = 8
    spec = pl.BlockSpec((heads, 64, 2 * DH), lambda i: (i, 0, 0))
    return pl.pallas_call(
        join_kernel,
        grid=(16 // heads,),
        out_shape=jax.ShapeDtypeStruct((16, 64, 6 * DH), bf16),
        in_specs=[spec, spec, pl.BlockSpec((2, heads, 64, DH), lambda i: (0, i, 0, 0))]
        + [ANYSPEC] * len(earlier),
        out_specs=pl.BlockSpec((heads, 64, 6 * DH), lambda i: (i, 0, 0)),
        compiler_params=params(56),
        name="join",
        cost_estimate=cost(1, 1),
    )(own, peer, queries, *earlier)


TILES = 2 * TOK // TILE
GRAD_SCRATCH = [
    pltpu.VMEM((3, DH, HALF), f32),
    pltpu.VMEM((TILES, TILE, 2 * DH), bf16),
    pltpu.SemaphoreType.DMA((TILES,)),
]


def token_copies(sides, kd, sem):
    copies = []
    for side, (ref, column) in enumerate(sides):
        for tile in range(TILES // 2):
            source = ref.at[pl.ds(tile * TILE, TILE), pl.ds(column, 2 * DH)]
            at = side * (TILES // 2) + tile
            copies.append(pltpu.make_async_copy(source, kd.at[at], sem.at[at]))
    return copies


def grad_body(kd, kd_sem, wb, acc_ref, out_refs, deep):
    acc_ref[...] = jnp.zeros_like(acc_ref)

    def tile(at, carry):
        pltpu.make_async_copy(kd.at[at], kd.at[at], kd_sem.at[at]).wait()
        key = kd[at, :, :DH]
        dout = kd[at, :, DH:]
        gate = dot(key, wb[0], ((1,), (0,)))
        up = dot(key, wb[1], ((1,), (0,)))
        dhid = dot(dout, wb[2], ((1,), (0,)))
        sigma = jax.nn.sigmoid(gate)
        active = gate * sigma
        hidden = (active * up).astype(bf16)
        d_up = (dhid * active).astype(bf16)
        d_gate = (dhid * up * sigma * (1.0 + gate * (1.0 - sigma))).astype(bf16)
        for index, (left, right) in enumerate(((key, d_gate), (key, d_up), (dout, hidden))):
            acc_ref[index] += dot(left, right, ((0,), (0,)))
        return carry

    lax.fori_loop(0, TILES, tile, 0)
    for far in range(4):
        cols = pl.ds(pl.multiple_of(((deep + far) & 3) * LANE, LANE), LANE)
        out_refs[far][...] = acc_ref[:, :, cols].astype(bf16)


def grad_kernel(place_ref, own_ref, peer_ref, wb_ref, *refs):
    out_refs, (acc_ref, kd, kd_sem, wb, wb_sem) = refs[:4], refs[4:]
    fetch = pltpu.make_async_copy(wb_ref.at[0], wb, wb_sem)
    fetch.start()
    copies = token_copies(((own_ref, 0), (peer_ref, 0)), kd, kd_sem)
    copies[0].start()
    fetch.wait()
    for copy in copies[1:]:
        copy.start()
    grad_body(kd, kd_sem, wb, acc_ref, out_refs, place_ref[1])


def grads(place, own, peer, both):
    return pl.pallas_call(
        grad_kernel,
        out_shape=[jax.ShapeDtypeStruct((3, DH, LANE), bf16)] * 4,
        in_specs=[SSPEC] + [HBMSPEC] * 3,
        out_specs=[VSPEC] * 4,
        scratch_shapes=GRAD_SCRATCH + [pltpu.VMEM((3, DH, HALF), bf16), pltpu.SemaphoreType.DMA(())],
        compiler_params=params(24),
        name="grads",
        cost_estimate=cost(12 * 2 * TOK * DH * HALF, 4 * MIB, 2 * TOK * HALF),
    )(place, own, peer, both)


NS_SCRATCH = [
    pltpu.VMEM((3, DH, FF), bf16),
    pltpu.VMEM((3, 8, DH, LANE), f32),
    pltpu.VMEM((2, 3, DH, HALF), bf16),
    pltpu.SemaphoreType.DMA(()),
]


def renew(weight, value, step):
    cand = weight - step * value.astype(f32)
    scale = jnp.sqrt(jnp.sum(weight * weight, axis=0, keepdims=True) + 1e-06) / jnp.sqrt(
        jnp.sum(cand * cand, axis=0, keepdims=True) + 1e-06
    )
    return cand * scale


def ns_body(grad, w_ref, step_ref, scratch, others, keep):
    ortho, weights, both, sem = scratch
    fetch = pltpu.make_async_copy(w_ref, weights, sem)
    fetch.start()
    for other in others:
        other.start()
    def begin(index, carry):
        total = None
        for half in range(2):
            for chunk in range(4):
                part = grad[half, chunk, index].astype(f32)
                part = part * part
                total = part if total is None else total + part
        total = jnp.sum(jnp.sum(total, axis=0, keepdims=True), axis=1, keepdims=True)
        norm = jnp.sqrt(total) + 1e-07
        for half in range(2):
            for chunk in range(4):
                at = (half * 4 + chunk) * LANE
                unit = (grad[half, chunk, index].astype(f32) / norm).astype(bf16)
                ortho[index, :, at : at + LANE] = unit
        return carry

    def iterate(step, carry):
        grams = [dot(ortho[i], ortho[i], ((1,), (1,))).astype(bf16) for i in range(3)]
        squares = [dot(gram, gram, ((1,), (0,))) for gram in grams]
        polys = [
            (coef_b * gram.astype(f32) + coef_c * square).astype(bf16) for gram, square in zip(grams, squares)
        ]
        for i in range(3):
            moved = dot(polys[i], ortho[i], ((1,), (0,)))
            ortho[i] = (coef_a * ortho[i].astype(f32) + moved).astype(bf16)
        return carry

    def update(index, carry):
        step = step_ref[0:1, 0:1]
        for chunk in range(8):
            value = ortho[index, :, chunk * LANE : (chunk + 1) * LANE]
            fresh = renew(weights[index, chunk], value, step)
            at = (chunk % 4) * LANE
            both[chunk // 4, index, :, at : at + LANE] = fresh.astype(bf16)
            if keep:
                weights[index, chunk] = fresh
        return carry

    lax.fori_loop(0, 3, begin, 0)
    lax.fori_loop(0, NS_STEPS, iterate, 0, unroll=True)
    fetch.wait()
    lax.fori_loop(0, 3, update, 0)


NS_FLOPS = 3 * 1510 * 10**6
BOTH = jax.ShapeDtypeStruct((2, 3, DH, HALF), bf16)


GRAD_PIECES = [pltpu.VMEM((2, 4, 3, DH, LANE), bf16), pltpu.SemaphoreType.DMA((8,))]


def load_pieces(g_refs, grad, sem, deep):
    pieces = []
    for i, ref in enumerate(g_refs):
        if len(g_refs) == 2:
            target = grad.at[i]
        else:
            target = grad.at[i // 4, (deep + i) & 3]
        pieces.append(pltpu.make_async_copy(ref, target, sem.at[i]))
    for piece in pieces:
        piece.start()
    for piece in pieces:
        piece.wait()
    return grad


def turn_kernel(*refs):
    place_ref, g_refs, w_ref, step_ref, rest_ref = refs[0], refs[1:3], *refs[3:6]
    both_ref, wnew_ref, out_refs, scratch = refs[6], refs[7], refs[8:12], refs[12:]
    ns_scratch, (acc_ref, kd, kd_sem), sem = scratch[:4], scratch[4:7], scratch[7]
    weights, both = ns_scratch[1], ns_scratch[2]
    grad = load_pieces(g_refs, *scratch[8:], place_ref[1])
    copies = token_copies(((rest_ref, 0), (rest_ref, 2 * DH)), kd, kd_sem)
    ns_body(grad, w_ref, step_ref, ns_scratch, copies, True)
    done = [
        pltpu.make_async_copy(both, both_ref, sem.at[0]),
        pltpu.make_async_copy(weights, wnew_ref, sem.at[1]),
    ]
    for copy in done:
        copy.start()
    grad_body(kd, kd_sem, both.at[0], acc_ref, out_refs, place_ref[1])
    for copy in done:
        copy.wait()


def turn(place, chunks, weight, step, rest):
    return pl.pallas_call(
        turn_kernel,
        out_shape=[BOTH, jax.ShapeDtypeStruct((3, 8, DH, LANE), f32)]
        + [jax.ShapeDtypeStruct((3, DH, LANE), bf16)] * 4,
        in_specs=[SSPEC] + [HBMSPEC] * 3 + [VSPEC, HBMSPEC],
        out_specs=[HBMSPEC] * 2 + [VSPEC] * 4,
        scratch_shapes=NS_SCRATCH + GRAD_SCRATCH + [pltpu.SemaphoreType.DMA((2,))] + GRAD_PIECES,
        compiler_params=params(56),
        name="turn",
        cost_estimate=cost(NS_FLOPS + 12 * 2 * TOK * DH * HALF, 14 * MIB, 2 * TOK * HALF),
    )(place, *chunks, weight, step, rest)


def query_half(queries, weights, half, acc_ref, out_ref, column):
    def tile(at, carry):
        rows = pl.ds(pl.multiple_of(at * TILE, TILE), TILE)
        query = queries[rows, :]
        gate = dot(query, weights[0], ((1,), (0,)))
        up = dot(query, weights[1], ((1,), (0,)))
        hidden = (gate * jax.nn.sigmoid(gate) * up).astype(bf16)
        part = dot(hidden, weights[2], ((1,), (1,)))
        if half:
            out_ref[rows, column : column + DH] = (acc_ref[rows, :] + part).astype(bf16)
        else:
            acc_ref[rows, :] = part
        return carry

    lax.fori_loop(0, TOK // TILE, tile, 0, unroll=True)


QUERY_SCRATCH = [pltpu.VMEM((TOK, DH), f32), pltpu.VMEM((TOK, DH), bf16), pltpu.SemaphoreType.DMA(())]


def query_kernel(column, rest_ref, both_ref, *refs):
    out_ref, acc_ref, queries, q_sem, both, sem = refs[-6:]
    copies = [pltpu.make_async_copy(both_ref.at[half], both.at[half], sem.at[half]) for half in range(2)]
    fetch = pltpu.make_async_copy(rest_ref.at[:, pl.ds(column, DH)], queries, q_sem)
    fetch.start()
    copies[0].start()
    fetch.wait()
    copies[0].wait()
    copies[1].start()
    query_half(queries, both.at[0], 0, acc_ref, out_ref, 0)
    copies[1].wait()
    query_half(queries, both.at[1], 1, acc_ref, out_ref, 0)


def forward(rest, both, column, *earlier):
    return pl.pallas_call(
        functools.partial(query_kernel, column),
        out_shape=jax.ShapeDtypeStruct((TOK, DH), bf16),
        in_specs=[HBMSPEC] * 2 + [ANYSPEC] * len(earlier),
        out_specs=VSPEC,
        scratch_shapes=QUERY_SCRATCH + [pltpu.VMEM((2, 3, DH, HALF), bf16), pltpu.SemaphoreType.DMA((2,))],
        compiler_params=params(56),
        name="forward",
        cost_estimate=cost(6 * TOK * DH * FF, 3 * MIB, TOK * FF),
    )(rest, both, *earlier)


def close_kernel(*refs):
    place_ref, g_refs, w_ref, step_ref, rest_ref = refs[0], refs[1:9], *refs[9:12]
    one_ref, two_ref, out_ref = refs[-13:-10]
    ns_scratch, pieces, (acc_ref, queries, q_sem), sem = refs[-10:-6], refs[-6:-4], refs[-4:-1], refs[-1]
    both = ns_scratch[2]
    fetch = pltpu.make_async_copy(rest_ref.at[:, pl.ds(5 * DH, DH)], queries, q_sem)
    ns_body(load_pieces(g_refs, *pieces, place_ref[1]), w_ref, step_ref, ns_scratch, [fetch], False)
    done = [
        pltpu.make_async_copy(both.at[0], one_ref, sem.at[0]),
        pltpu.make_async_copy(both.at[1], two_ref, sem.at[1]),
    ]
    for copy in done:
        copy.start()
    fetch.wait()
    for half in range(2):
        query_half(queries, both.at[half], half, acc_ref, out_ref, 0)
    for copy in done:
        copy.wait()


def close(place, chunks, weight, step, rest, *earlier):
    return pl.pallas_call(
        close_kernel,
        out_shape=[jax.ShapeDtypeStruct((3, DH, HALF), bf16)] * 2 + [jax.ShapeDtypeStruct((TOK, DH), bf16)],
        in_specs=[SSPEC] + [HBMSPEC] * 9 + [VSPEC, HBMSPEC] + [ANYSPEC] * len(earlier),
        out_specs=[HBMSPEC, HBMSPEC, VSPEC],
        scratch_shapes=NS_SCRATCH + GRAD_PIECES + QUERY_SCRATCH + [pltpu.SemaphoreType.DMA((2,))],
        compiler_params=params(56),
        name="close",
        cost_estimate=cost(NS_FLOPS + 6 * TOK * DH * FF, 10 * MIB, TOK * FF),
    )(place, *chunks, weight, step, rest, *earlier)


def prep_kernel(place_ref, *refs):
    local, other, step_ref, step_other_ref = refs[:3], refs[3:6], refs[6], refs[7]
    wrot_ref, both_ref, step_out_ref, weights, sem, out_sem = refs[8:]
    core, mine, row = place_ref[0], place_ref[2], place_ref[3]
    step_out_ref[...] = jnp.where(mine == 1, step_ref[...], step_other_ref[...])

    def fetch(sources):
        copies = []
        for index in range(3):
            for chunk in range(8):
                block = (core ^ (chunk // 4)) * 4 + chunk % 4
                cols = pl.ds(pl.multiple_of(block * LANE, LANE), LANE)
                copies.append(
                    pltpu.make_async_copy(
                        sources[index].at[row, :, cols], weights.at[index, chunk], sem.at[index, chunk]
                    )
                )
        return copies

    @pl.when(mine == 1)
    def _():
        for copy in fetch(local):
            copy.start()

    @pl.when(mine != 1)
    def _():
        for copy in fetch(other):
            copy.start()

    def cast(index, carry):
        for chunk in range(8):
            pltpu.make_async_copy(weights.at[index, chunk], weights.at[index, chunk], sem.at[index, chunk]).wait()
            at = (chunk % 4) * LANE
            both_ref[chunk // 4, index, :, at : at + LANE] = weights[index, chunk].astype(bf16)
        return carry

    lax.fori_loop(0, 3, cast, 0)
    copy = pltpu.make_async_copy(weights, wrot_ref, out_sem)
    copy.start()
    copy.wait()


def prepare(place, local, other, step, step_other):
    return pl.pallas_call(
        prep_kernel,
        out_shape=(
            jax.ShapeDtypeStruct((3, 8, DH, LANE), f32),
            BOTH,
            jax.ShapeDtypeStruct((8, LANE), f32),
        ),
        in_specs=[SSPEC] + [HBMSPEC] * 6 + [VSPEC] * 2,
        out_specs=(HBMSPEC, VSPEC, VSPEC),
        scratch_shapes=[
            pltpu.VMEM((3, 8, DH, LANE), f32),
            pltpu.SemaphoreType.DMA((3, 8)),
            pltpu.SemaphoreType.DMA(()),
        ],
        compiler_params=params(56),
        name="prepare",
        cost_estimate=cost(1, 1),
    )(place, *local, *other, step, step_other)


def final_kernel(place_ref, *refs):
    near, sent, outs, result_ref = refs[:8], refs[8:10], refs[10:13], refs[13]
    buf, wide, late, wide_late, in_sem, out_sem, late_sem, result_sem = refs[14:]
    core, row = place_ref[0], place_ref[4]
    slots = [(head, half) for head in range(2) for half in range(2)]
    fetches = [pltpu.make_async_copy(sent[i], late.at[i], late_sem.at[i]) for i in range(GROUPS)]
    for fetch in fetches:
        fetch.start()

    def start(ref, slot):
        pltpu.make_async_copy(ref, buf.at[slot], in_sem.at[slot]).start()

    for slot, (head, half) in enumerate(slots):
        away = (row - 2 * core - head) & 3
        flip = core ^ half
        for far in range(4):
            for side in range(2):
                pl.when((away == far) & (flip == side))(functools.partial(start, near[2 * far + side], slot))
    done = []
    for group in range(GROUPS):
        fetches[group].wait()
        wide_late[group] = late[group].astype(f32)
        done.append(pltpu.make_async_copy(wide_late.at[group], result_ref.at[group], result_sem.at[group]))
        done[-1].start()

    def write(slot, carry):
        head, half = slot // 2, slot % 2
        pltpu.make_async_copy(buf.at[slot], buf.at[slot], in_sem.at[slot]).wait()
        for index in range(3):
            wide[slot, index] = buf[slot, index].astype(f32)
            cols = pl.ds(pl.multiple_of(half * HALF, HALF), HALF)
            target = outs[index].at[head, :, cols]
            pltpu.make_async_copy(wide.at[slot, index], target, out_sem.at[slot, index]).start()
        return carry

    lax.fori_loop(0, 4, write, 0)
    for slot, (head, half) in enumerate(slots):
        for index in range(3):
            target = outs[index].at[head, :, pl.ds(half * HALF, HALF)]
            done.append(pltpu.make_async_copy(wide.at[slot, index], target, out_sem.at[slot, index]))
    for copy in done:
        copy.wait()


def finish(place, near, sent):
    return pl.pallas_call(
        final_kernel,
        out_shape=[jax.ShapeDtypeStruct((2, DH, FF), f32)] * 3
        + [jax.ShapeDtypeStruct((GROUPS, 16, 64, DH), f32)],
        in_specs=[SSPEC] + [HBMSPEC] * 10,
        out_specs=[HBMSPEC] * 4,
        scratch_shapes=[
            pltpu.VMEM((4, 3, DH, HALF), bf16),
            pltpu.VMEM((4, 3, DH, HALF), f32),
            pltpu.VMEM((GROUPS, 16, 64, DH), bf16),
            pltpu.VMEM((GROUPS, 16, 64, DH), f32),
            pltpu.SemaphoreType.DMA((4,)),
            pltpu.SemaphoreType.DMA((4, 3)),
            pltpu.SemaphoreType.DMA((GROUPS,)),
            pltpu.SemaphoreType.DMA((GROUPS,)),
        ],
        compiler_params=params(56),
        name="finish",
        cost_estimate=cost(10**6, 15 * MIB),
    )(place, *near, *sent)


def ring(far):
    return [(i, (i + far) % 4) for i in range(4)]


SWAP = [(0, 1), (1, 0)]


def swap(value):
    return lax.ppermute(value, "c", SWAP)


def sum_up(partial):
    received = [lax.ppermute(partial[far], "z", ring(far)) for far in (2, 1, 3)]
    total = partial[0].astype(f32)
    for part in received:
        total = total + part.astype(f32)
    return total.astype(bf16)


def gather(value):
    whole = lax.all_gather(value, "z")
    return whole, swap(whole)


def gather_direct(value):
    far2, far1, far3 = [lax.ppermute(value, "z", ring(4 - far)) for far in (2, 1, 3)]
    chunks = [value, far1, far2, far3]
    return chunks + [swap(chunk) for chunk in chunks]


def y_pairs(start, end):
    return [(2 * ((y + start) % 4) + y // 2, 2 * ((y + end) % 4) + y // 2) for y in range(4)]


def shards(queries, keys, values, rates, step_sizes, w_gate, w_up, w_down):
    z, y, c = lax.axis_index("z"), lax.axis_index("y"), lax.axis_index("c")
    exchange = functools.partial(
        lax.all_to_all, axis_name=("x", "y"), split_axis=0, concat_axis=0, tiled=True
    )
    packed, own = pack(keys, values, rates)
    first = exchange(packed).reshape(TOK, 2 * DH)
    mine = (c == y // 2).astype(jnp.int32)
    stored = (w_gate, w_up, w_down)
    step_local = jnp.broadcast_to(lax.dynamic_index_in_dim(step_sizes, y % 2, 0), (8, LANE))
    place = jnp.stack([c, z, mine, y % 2, y]).astype(jnp.int32)
    others = [swap(w) for w in stored]
    weights, both, step = prepare(place, stored, others, step_local, swap(step_local))
    second = join(own, swap(own), queries, step)
    first = after(first, step, second)
    rest = exchange(after(second, first)).reshape(TOK, 6 * DH)

    chunks = gather(sum_up(grads(place, first, swap(first), both)))
    both, weights, *partial = turn(place, chunks, weights, step, rest)

    early = exchange(forward(rest, both, 4 * DH, partial[0]).reshape(16, 64, DH))
    chunks = gather_direct(sum_up(partial))
    one, two, result = close(place, chunks, weights, step, rest, early)
    move = functools.partial(lax.ppermute, axis_name=("y", "c"))
    up, down = move(one, perm=y_pairs(0, 1)), move(two, perm=y_pairs(0, 3))
    near = [one, two, up, move(two, perm=y_pairs(0, 1))]
    near += [move(up, perm=y_pairs(1, 2)), move(down, perm=y_pairs(3, 2))]
    near += [move(one, perm=y_pairs(0, 3)), down]
    late = exchange(result.reshape(16, 64, DH))
    gate, up, down, outputs = finish(place, near, (early, late))
    return (outputs, gate, up, down)


def solution(mesh):
    grid = Mesh(mesh.devices.reshape(4, 4, 4, 2), ("z", "y", "x", "c"))
    tokens = ("z", "y", "x", "c")
    heads = ("x", "c")
    return jax.shard_map(
        shards,
        mesh=grid,
        in_specs=(
            P(None, None, tokens, None),
            P(None, None, tokens, None),
            P(None, None, tokens, None),
            P(None, None, tokens),
            P(heads),
            P(heads, None, None),
            P(heads, None, None),
            P(heads, None, None),
        ),
        out_specs=(
            P(None, None, tokens, None),
            P(heads, None, None),
            P(heads, None, None),
            P(heads, None, None),
        ),
        check_vma=False,
    )
```

time: 556 us -> 186 us (0.33)
  the two profiles are of different devices: /device:TPU:1 before, /device:TPU:20 now
where the time goes in v1:
time: 186 us; the launch traced here: 183 us
  Pallas kernels  58.8 us (32%)
  starting transfers between devices  47.7 us (26%)
  blocking collectives  34.8 us (19%)
  waiting for transfers between devices  33 us (18%)
  local copies, waits for them, and re-layouts  6.9 us (4%)
    all_to_all x1, blocking collectives, shards(): late = exchange(result.reshape(16, 64, DH))  21.4 us
    pallas_call x1, Pallas kernels, turn(): pl.pallas_call(turn_kernel, out_shape=[BOTH, jax.ShapeDtypeStruct((3, 8,...  17 us
    all_gather x1, blocking collectives, gather(): whole = lax.all_gather(value, 'z')  13.5 us
    pallas_call x1, Pallas kernels, close(): pl.pallas_call(close_kernel, out_shape=[jax.ShapeDtypeStruct((3, DH, HALF...  13.2 us
    ppermute x6, starting transfers between devices, sum_up(): received = [lax.ppermute(partial[far], 'z', ring(far)) for far in (2, 1, 3)]  12.3 us
    ppermute x2, waiting for transfers between devices, shards(): up, down = (move(one, perm=y_pairs(0, 1)), move(two, perm=y_pairs(0, 3)))  10.1 us
    all_to_all x1, starting transfers between devices, shards(): rest = exchange(after(second, first)).reshape(TOK, 6 * DH)  8.3 us
    ppermute x3, waiting for transfers between devices, gather_direct(): lax.ppermute(value, 'z', ring(4 - far))  7.65 us
  transfers between devices with their start and end apart: 29, of which 13 were waited for; matrix products, arithmetic and copies ran while one was open for 1% of the time, Pallas kernels for 12%

profile of v1, /device:TPU:20, one launch (start us, length us, event | category | flops | bytes accessed | tf_op | source)
XLA Modules:
  0.0 182.7 jit_solution(17355888863551542697)
XLA Ops:
  1.3 2.7 %pack.1 = (bf16[16,64,512]{2,1,0:T(8,128)(2,1)}, bf16[16,64,512]{2,1,0:T(8,128)(2,1)}) custom-call(bf16[2,16,64,256]{3,2,1,0:T(8,128)(2,1)} %key_ref.1, bf16[2,16,64,256]{3,2,1,0:T(8,128)(2,1)} %value_ref.1, bf16[2,16,64]{2,1,0:T(8,128)(2,1)} %rate_ref.1), custom_call_target="tpu_custom_call" | custom-call | flops 1 | bytes 1 | tf_op jit(solution)/shard_map/pack/pallas_call | solution.py:60
  4.4 7.2 %all-to-all-start = ((bf16[16,64,512]{2,1,0:T(8,128)(2,1)}), bf16[16,64,512]{2,1,0:T(8,128)(2,1)S(1)}, u32[]{:S(2)}, u32[]{:S(2)}) async-start(bf16[16,64,512]{2,1,0:T(8,128)(2,1)} %get-tuple-element.28), calls=%async_computation | async-start | bytes 2097152 | tf_op jit(solution)/shard_map/all_to_all | solution.py:535
  15.5 5.7 %prepare.1 = (f32[3,8,256,128]{3,2,1,0:T(8,128)}, bf16[2,3,256,512]{3,2,1,0:T(8,128)(2,1)}, f32[8,128]{1,0:T(8,128)}) custom-call(s32[5]{0:T(128)} %stack.27.place_ref.refs_0_, f32[2,256,1024]{2,1,0:T(8,128)} %refs_0_.1, f32[2,256,1024]{2,1,0:T(8,128)} %refs_1_.1, f32[2,256,1024]{2,1,0:T(8,128)} %refs_2_.1, f32[2,256,1024]{2,1,0:T(8,128)} %copy-done.2, ...), custom_call_target="tpu_custom_call" | custom-call | flops 1 | bytes 1 | tf_op jit(solution)/shard_map/prepare/pallas_call | solution.py:408
  21.2 3.2 %join.1 = bf16[16,64,1536]{2,1,0:T(8,128)(2,1)} custom-call(bf16[16,64,512]{2,1,0:T(8,128)(2,1)} %get-tuple-element.30.own_ref, bf16[16,64,512]{2,1,0:T(8,128)(2,1)} %collective-permute-done.4.peer_ref, bf16[2,16,64,256]{3,2,1,0:T(8,128)(2,1)} %queries_ref.1, f32[8,128]{1,0:T(8,128)} %get-tuple-element.29.refs_0_.refs_4_.refs_10_), custom_call_target="tpu_custom_call" | custom-call | flops 1 | bytes 1 | tf_op jit(solution)/shard_map/join/pallas_call | solution.py:83
  25.9 8.3 %all-to-all-start.1 = ((bf16[16,64,1536]{2,1,0:T(8,128)(2,1)}), bf16[16,64,1536]{2,1,0:T(8,128)(2,1)}, u32[]{:S(2)}, u32[]{:S(2)}) async-start(bf16[16,64,1536]{2,1,0:T(8,128)(2,1)} %join.1), calls=%async_computation.1 | async-start | bytes 6291456 | tf_op jit(solution)/shard_map/all_to_all | solution.py:544
  34.2 2.7 %collective-permute-done.5.peer_ref = bf16[1024,512]{1,0:T(8,128)(2,1)S(1)} collective-permute-done((bf16[1024,512]{1,0:T(8,128)(2,1)S(1)}, bf16[1024,512]{1,0:T(8,128)(2,1)S(1)}, u32[]{:S(2)}, u32[]{:S(2)}) %collective-permute-start.5) | collective-permute-done | bytes 1048608 | tf_op jit(solution)/shard_map/ppermute | solution.py:503
  36.9 6.5 %grads.1 = (bf16[3,256,128]{2,1,0:T(8,128)(2,1)S(1)}, bf16[3,256,128]{2,1,0:T(8,128)(2,1)S(1)}, bf16[3,256,128]{2,1,0:T(8,128)(2,1)S(1)}, bf16[3,256,128]{2,1,0:T(8,128)(2,1)S(1)}) custom-call(s32[5]{0:T(128)S(1)} %copy-done, bf16[1024,512]{1,0:T(8,128)(2,1)S(1)} %bitcast.12, bf16[1024,512]{1,0:T(8,128)(2,1)S(1)} %collective-permute-done.5.peer_ref, ...), custom_call_target="tpu_custom_call" | custom-call | flops 3221225472 | bytes 4194304 | tf_op jit(solution)/shard_map/grads/pallas_call | solution.py:152
  43.4 4.0 %collective-permute-start.6 = (bf16[3,256,128]{2,1,0:T(8,128)(2,1)S(1)}, bf16[3,256,128]{2,1,0:T(8,128)(2,1)S(1)}, u32[]{:S(2)}, u32[]{:S(2)}) collective-permute-start(bf16[3,256,128]{2,1,0:T(8,128)(2,1)S(1)} %get-tuple-element.34), channel_id=1, source_target_pairs={{0,64},{32,96},{64,0},{96,32},{1,65},{33,97},{65,1},{97,33},{2,66}... | collective-permute-start | bytes 589832 | tf_op jit(solution)/shard_map/ppermute | solution.py:507
  48.3 2.2 %collective-permute-start.8 = (bf16[3,256,128]{2,1,0:T(8,128)(2,1)S(1)}, bf16[3,256,128]{2,1,0:T(8,128)(2,1)S(1)}, u32[]{:S(2)}, u32[]{:S(2)}) collective-permute-start(bf16[3,256,128]{2,1,0:T(8,128)(2,1)S(1)} %get-tuple-element.36), channel_id=1, source_target_pairs={{0,96},{32,0},{64,32},{96,64},{1,97},{33,1},{65,33},{97,65},{2,98}... | collective-permute-start | bytes 589832 | tf_op jit(solution)/shard_map/ppermute | solution.py:507
  50.6 2.4 %collective-permute-done.6 = bf16[3,256,128]{2,1,0:T(8,128)(2,1)S(1)} collective-permute-done((bf16[3,256,128]{2,1,0:T(8,128)(2,1)S(1)}, bf16[3,256,128]{2,1,0:T(8,128)(2,1)S(1)}, u32[]{:S(2)}, u32[]{:S(2)}) %collective-permute-start.6) | collective-permute-done | bytes 196640 | tf_op jit(solution)/shard_map/ppermute | solution.py:507
  53.0 3.7 %collective-permute-done.7 = bf16[3,256,128]{2,1,0:T(8,128)(2,1)S(1)} collective-permute-done((bf16[3,256,128]{2,1,0:T(8,128)(2,1)S(1)}, bf16[3,256,128]{2,1,0:T(8,128)(2,1)S(1)}, u32[]{:S(2)}, u32[]{:S(2)}) %collective-permute-start.7) | collective-permute-done | bytes 196640 | tf_op jit(solution)/shard_map/ppermute | solution.py:507
  57.6 13.5 %all-gather = bf16[12,256,128]{2,1,0:T(8,128)(2,1)S(1)} all-gather(bf16[3,256,128]{2,1,0:T(8,128)(2,1)S(1)} %add_convert_fusion.1), channel_id=2, replica_groups=mesh['z'=4,'y'=4,'x'=4,'c'=2] {'z'}, dimensions={0}, use_global_device_ids=true | all-gather | bytes 983040 | tf_op jit(solution)/shard_map/all_gather | solution.py:515
  71.1 2.3 %collective-permute-done.9.refs_2_ = bf16[4,3,256,128]{3,2,1,0:T(8,128)(2,1)S(1)} collective-permute-done((bf16[4,3,256,128]{3,2,1,0:T(8,128)(2,1)S(1)}, bf16[4,3,256,128]{3,2,1,0:T(8,128)(2,1)S(1)}, u32[]{:S(2)}, u32[]{:S(2)}) %collective-permute-start.9) | collective-permute-done | bytes 786464 | tf_op jit(solution)/shard_map/ppermute | solution.py:503
  74.2 17.0 %turn.1 = (bf16[2,3,256,512]{3,2,1,0:T(8,128)(2,1)}, f32[3,8,256,128]{3,2,1,0:T(8,128)}, bf16[3,256,128]{2,1,0:T(8,128)(2,1)}, bf16[3,256,128]{2,1,0:T(8,128)(2,...) custom-call(s32[5]{0:T(128)} %stack.27.place_ref.refs_0_, bf16[4,3,256,128]{3,2,1,0:T(8,128)(2,1)} %bitcast.14, ...), custom_call_target="tpu_custom_call" | custom-call | flops 7751225344 | bytes 14680064 | tf_op jit(solution)/shard_map/turn/pallas_call | solution.py:272
  93.1 2.6 %collective-permute-start.11 = (bf16[3,256,128]{2,1,0:T(8,128)(2,1)}, bf16[3,256,128]{2,1,0:T(8,128)(2,1)S(1)}, u32[]{:S(2)}, u32[]{:S(2)}) collective-permute-start(bf16[3,256,128]{2,1,0:T(8,128)(2,1)} %get-tuple-element.41), channel_id=1, source_target_pairs={{0,32},{32,64},{64,96},{96,0},{1,33},{33,65},{65,97},{97,1},{2,34}... | collective-permute-start | bytes 589832 | tf_op jit(solution)/shard_map/ppermute | solution.py:507
  96.4 4.4 %forward.1 = bf16[1024,256]{1,0:T(8,128)(2,1)} custom-call(bf16[1024,1536]{1,0:T(8,128)(2,1)} %bitcast.8.refs_5_.rest_ref.refs_11_, bf16[2,3,256,512]{3,2,1,0:T(8,128)(2,1)} %get-tuple-element.44.both_ref, bf16[3,256,128]{2,1,0:T(8,128)(2,1)} %get-tuple-element.39.refs_0_), custom_call_target="tpu_custom_call" | custom-call | flops 1610612736 | bytes 3145728 | tf_op jit(solution)/shard_map/forward/pallas_call | solution.py:320
  100.8 7.2 %all-to-all-start.2 = ((bf16[16,64,256]{2,1,0:T(8,128)(2,1)}), bf16[16,64,256]{2,1,0:T(8,128)(2,1)S(1)}, u32[]{:S(2)}, u32[]{:S(2)}) async-start(bf16[16,64,256]{2,1,0:T(8,128)(2,1)} %bitcast.15), calls=%async_computation.2 | async-start | bytes 1048576 | tf_op jit(solution)/shard_map/all_to_all | solution.py:549
  109.6 2.1 %collective-permute-start.14 = (bf16[3,256,128]{2,1,0:T(8,128)(2,1)S(1)}, bf16[3,256,128]{2,1,0:T(8,128)(2,1)S(1)}, u32[]{:S(2)}, u32[]{:S(2)}) collective-permute-start(bf16[3,256,128]{2,1,0:T(8,128)(2,1)S(1)} %add_convert_fusion.refs_1_), channel_id=1, source_target_pairs={{0,64},{32,96},{64,0},{96,32},{1,65},{33,97},{65,1},{97,33},{2,66}... | collective-permute-start | bytes 589832 | tf_op jit(solution)/shard_map/ppermute | solution.py:520
  112.4 5.2 %collective-permute-done.15.refs_4_ = bf16[3,256,128]{2,1,0:T(8,128)(2,1)S(1)} collective-permute-done((bf16[3,256,128]{2,1,0:T(8,128)(2,1)S(1)}, bf16[3,256,128]{2,1,0:T(8,128)(2,1)S(1)}, u32[]{:S(2)}, u32[]{:S(2)}) %collective-permute-start.15) | collective-permute-done | bytes 196640 | tf_op jit(solution)/shard_map/ppermute | solution.py:520
  122.2 13.2 %close.1 = (bf16[3,256,512]{2,1,0:T(8,128)(2,1)}, bf16[3,256,512]{2,1,0:T(8,128)(2,1)}, bf16[1024,256]{1,0:T(8,128)(2,1)}) custom-call(s32[5]{0:T(128)} %stack.27.place_ref.refs_0_, bf16[3,256,128]{2,1,0:T(8,128)(2,1)} %copy-done.11, bf16[3,256,128]{2,1,0:T(8,128)(2,1)} %copy-done.18, bf16[3,256,128]{2,1,0:T(8,128)(2,1)} %copy-done.17, ...), custom_call_target="tpu_custom_call" | custom-call | flops 6140612608 | bytes 10485760 | tf_op jit(solution)/shard_map/close/pallas_call | solution.py:353
  139.4 10.1 %collective-permute-done.20.refs_2_ = bf16[3,256,512]{2,1,0:T(8,128)(2,1)S(1)} collective-permute-done((bf16[3,256,512]{2,1,0:T(8,128)(2,1)}, bf16[3,256,512]{2,1,0:T(8,128)(2,1)S(1)}, u32[]{:S(2)}, u32[]{:S(2)}) %collective-permute-start.20) | collective-permute-done | bytes 786464 | tf_op jit(solution)/shard_map/ppermute | solution.py:553
  149.5 1.9 %collective-permute-start.22 = (bf16[3,256,512]{2,1,0:T(8,128)(2,1)S(1)}, bf16[3,256,512]{2,1,0:T(8,128)(2,1)S(1)}, u32[]{:S(2)}, u32[]{:S(2)}) collective-permute-start(bf16[3,256,512]{2,1,0:T(8,128)(2,1)S(1)} %collective-permute-done.20.refs_2_), channel_id=1, source_target_pairs={{8,16},{16,24},{25,1},{1,9},{10,18},{18,26},{27,3},{3,11},{12,20},... | collective-permute-start | bytes 2359304 | tf_op jit(solution)/shard_map/ppermute | solution.py:555
  152.7 21.4 %all_to_all.20.refs_9_ = bf16[16,64,256]{2,1,0:T(8,128)(2,1)} all-to-all(bf16[16,64,256]{2,1,0:T(8,128)(2,1)} %bitcast.16), channel_id=1, replica_groups=mesh['z'=4,'y'=4,'x'=4,'c'=2] {'x','y'}, dimensions={0} | all-to-all | bytes 1048576 | tf_op jit(solution)/shard_map/all_to_all | solution.py:557
  176.4 6.2 %finish.1 = (f32[2,256,1024]{2,1,0:T(8,128)}, f32[2,256,1024]{2,1,0:T(8,128)}, f32[2,256,1024]{2,1,0:T(8,128)}, f32[2,16,64,256]{3,2,1,0:T(8,128)}) custom-call(s32[5]{0:T(128)} %stack.27.place_ref.refs_0_, bf16[3,256,512]{2,1,0:T(8,128)(2,1)} %get-tuple-element.45.refs_0_, bf16[3,256,512]{2,1,0:T(8,128)(2,1)} %get-tuple-element.46.refs_1_, ...), custom_call_target="tpu_custom_call" | custom-call | flops 1000000 | bytes 15728640 | tf_op jit(solution)/shard_map/finish/pallas_call | solution.py:473
  (97 shorter events, 25.9 us)
Async XLA Ops:
  0.6 13.5 %collective-permute-start = (f32[2,256,1024]{2,1,0:T(8,128)}, f32[2,256,1024]{2,1,0:T(8,128)S(1)}, u32[]{:S(2)}, u32[]{:S(2)}) collective-permute-start(f32[2,256,1024]{2,1,0:T(8,128)} %refs_0_.1), channel_id=1, source_target_pairs={{0,1},{1,0},{2,3},{3,2},{4,5},{5,4},{6,7},{7,6},{8,9},{9,8},{10,11... | collective-permute-start | bytes 6291464 | tf_op jit(solution)/shard_map/ppermute | solution.py:503
  0.7 13.4 %collective-permute-start.1 = (f32[2,256,1024]{2,1,0:T(8,128)}, f32[2,256,1024]{2,1,0:T(8,128)}, u32[]{:S(2)}, u32[]{:S(2)}) collective-permute-start(f32[2,256,1024]{2,1,0:T(8,128)} %refs_1_.1), channel_id=1, source_target_pairs={{0,1},{1,0},{2,3},{3,2},{4,5},{5,4},{6,7},{7,6},{8,9},{9,8},{10,11... | collective-permute-start | bytes 6291464 | tf_op jit(solution)/shard_map/ppermute | solution.py:503
  1.2 12.9 %collective-permute-start.2 = (f32[2,256,1024]{2,1,0:T(8,128)}, f32[2,256,1024]{2,1,0:T(8,128)}, u32[]{:S(2)}, u32[]{:S(2)}) collective-permute-start(f32[2,256,1024]{2,1,0:T(8,128)} %refs_2_.1), channel_id=1, source_target_pairs={{0,1},{1,0},{2,3},{3,2},{4,5},{5,4},{6,7},{7,6},{8,9},{9,8},{10,11... | collective-permute-start | bytes 6291464 | tf_op jit(solution)/shard_map/ppermute | solution.py:503
  4.0 17.2 %collective-permute-start.4 = (bf16[16,64,512]{2,1,0:T(8,128)(2,1)}, bf16[16,64,512]{2,1,0:T(8,128)(2,1)}, u32[]{:S(2)}, u32[]{:S(2)}) collective-permute-start(bf16[16,64,512]{2,1,0:T(8,128)(2,1)} %get-tuple-element.30.own_ref), channel_id=1, source_target_pairs={{0,1},{1,0},{2,3},{3,2},{4,5},{5,4},{6,7},{7,6},{8,9},{9,8},{10,11... | collective-permute-start | bytes 3145736 | tf_op jit(solution)/shard_map/ppermute | solution.py:503
  4.4 21.5 %all-to-all-start = ((bf16[16,64,512]{2,1,0:T(8,128)(2,1)}), bf16[16,64,512]{2,1,0:T(8,128)(2,1)S(1)}, u32[]{:S(2)}, u32[]{:S(2)}) async-start(bf16[16,64,512]{2,1,0:T(8,128)(2,1)} %get-tuple-element.28), calls=%async_computation | async-start | bytes 2097152 | tf_op jit(solution)/shard_map/all_to_all | solution.py:535
  25.9 47.5 %all-to-all-start.1 = ((bf16[16,64,1536]{2,1,0:T(8,128)(2,1)}), bf16[16,64,1536]{2,1,0:T(8,128)(2,1)}, u32[]{:S(2)}, u32[]{:S(2)}) async-start(bf16[16,64,1536]{2,1,0:T(8,128)(2,1)} %join.1), calls=%async_computation.1 | async-start | bytes 6291456 | tf_op jit(solution)/shard_map/all_to_all | solution.py:544
  34.2 2.7 %collective-permute-start.5 = (bf16[1024,512]{1,0:T(8,128)(2,1)S(1)}, bf16[1024,512]{1,0:T(8,128)(2,1)S(1)}, u32[]{:S(2)}, u32[]{:S(2)}) collective-permute-start(bf16[1024,512]{1,0:T(8,128)(2,1)S(1)} %bitcast.11), channel_id=1, source_target_pairs={{0,1},{1,0},{2,3},{3,2},{4,5},{5,4},{6,7},{7,6},{8,9},{9,8},{10,11... | collective-permute-start | bytes 3145736 | tf_op jit(solution)/shard_map/ppermute | solution.py:503
  43.4 9.6 %collective-permute-start.6 = (bf16[3,256,128]{2,1,0:T(8,128)(2,1)S(1)}, bf16[3,256,128]{2,1,0:T(8,128)(2,1)S(1)}, u32[]{:S(2)}, u32[]{:S(2)}) collective-permute-start(bf16[3,256,128]{2,1,0:T(8,128)(2,1)S(1)} %get-tuple-element.34), channel_id=1, source_target_pairs={{0,64},{32,96},{64,0},{96,32},{1,65},{33,97},{65,1},{97,33},{2,66}... | collective-permute-start | bytes 589832 | tf_op jit(solution)/shard_map/ppermute | solution.py:507
  47.3 9.4 %collective-permute-start.7 = (bf16[3,256,128]{2,1,0:T(8,128)(2,1)S(1)}, bf16[3,256,128]{2,1,0:T(8,128)(2,1)S(1)}, u32[]{:S(2)}, u32[]{:S(2)}) collective-permute-start(bf16[3,256,128]{2,1,0:T(8,128)(2,1)S(1)} %get-tuple-element.35), channel_id=1, source_target_pairs={{0,32},{32,64},{64,96},{96,0},{1,33},{33,65},{65,97},{97,1},{2,34}... | collective-permute-start | bytes 589832 | tf_op jit(solution)/shard_map/ppermute | solution.py:507
  48.3 9.1 %collective-permute-start.8 = (bf16[3,256,128]{2,1,0:T(8,128)(2,1)S(1)}, bf16[3,256,128]{2,1,0:T(8,128)(2,1)S(1)}, u32[]{:S(2)}, u32[]{:S(2)}) collective-permute-start(bf16[3,256,128]{2,1,0:T(8,128)(2,1)S(1)} %get-tuple-element.36), channel_id=1, source_target_pairs={{0,96},{32,0},{64,32},{96,64},{1,97},{33,1},{65,33},{97,65},{2,98}... | collective-permute-start | bytes 589832 | tf_op jit(solution)/shard_map/ppermute | solution.py:507
  91.3 16.7 %collective-permute-start.10 = (bf16[3,256,128]{2,1,0:T(8,128)(2,1)}, bf16[3,256,128]{2,1,0:T(8,128)(2,1)S(1)}, u32[]{:S(2)}, u32[]{:S(2)}) collective-permute-start(bf16[3,256,128]{2,1,0:T(8,128)(2,1)} %get-tuple-element.40), channel_id=1, source_target_pairs={{0,64},{32,96},{64,0},{96,32},{1,65},{33,97},{65,1},{97,33},{2,66}... | collective-permute-start | bytes 589832 | tf_op jit(solution)/shard_map/ppermute | solution.py:507
  93.1 14.9 %collective-permute-start.11 = (bf16[3,256,128]{2,1,0:T(8,128)(2,1)}, bf16[3,256,128]{2,1,0:T(8,128)(2,1)S(1)}, u32[]{:S(2)}, u32[]{:S(2)}) collective-permute-start(bf16[3,256,128]{2,1,0:T(8,128)(2,1)} %get-tuple-element.41), channel_id=1, source_target_pairs={{0,32},{32,64},{64,96},{96,0},{1,33},{33,65},{65,97},{97,1},{2,34}... | collective-permute-start | bytes 589832 | tf_op jit(solution)/shard_map/ppermute | solution.py:507
  95.7 12.3 %collective-permute-start.12 = (bf16[3,256,128]{2,1,0:T(8,128)(2,1)}, bf16[3,256,128]{2,1,0:T(8,128)(2,1)S(1)}, u32[]{:S(2)}, u32[]{:S(2)}) collective-permute-start(bf16[3,256,128]{2,1,0:T(8,128)(2,1)} %get-tuple-element.42), channel_id=1, source_target_pairs={{0,96},{32,0},{64,32},{96,64},{1,97},{33,1},{65,33},{97,65},{2,98}... | collective-permute-start | bytes 589832 | tf_op jit(solution)/shard_map/ppermute | solution.py:507
  100.8 19.3 %all-to-all-start.2 = ((bf16[16,64,256]{2,1,0:T(8,128)(2,1)}), bf16[16,64,256]{2,1,0:T(8,128)(2,1)S(1)}, u32[]{:S(2)}, u32[]{:S(2)}) async-start(bf16[16,64,256]{2,1,0:T(8,128)(2,1)} %bitcast.15), calls=%async_computation.2 | async-start | bytes 1048576 | tf_op jit(solution)/shard_map/all_to_all | solution.py:549
  108.2 9.5 %collective-permute-start.15 = (bf16[3,256,128]{2,1,0:T(8,128)(2,1)S(1)}, bf16[3,256,128]{2,1,0:T(8,128)(2,1)S(1)}, u32[]{:S(2)}, u32[]{:S(2)}) collective-permute-start(bf16[3,256,128]{2,1,0:T(8,128)(2,1)S(1)} %add_convert_fusion.refs_1_), channel_id=1, source_target_pairs={{0,32},{32,64},{64,96},{96,0},{1,33},{33,65},{65,97},{97,1},{2,34}... | collective-permute-start | bytes 589832 | tf_op jit(solution)/shard_map/ppermute | solution.py:520
  109.6 9.8 %collective-permute-start.14 = (bf16[3,256,128]{2,1,0:T(8,128)(2,1)S(1)}, bf16[3,256,128]{2,1,0:T(8,128)(2,1)S(1)}, u32[]{:S(2)}, u32[]{:S(2)}) collective-permute-start(bf16[3,256,128]{2,1,0:T(8,128)(2,1)S(1)} %add_convert_fusion.refs_1_), channel_id=1, source_target_pairs={{0,64},{32,96},{64,0},{96,32},{1,65},{33,97},{65,1},{97,33},{2,66}... | collective-permute-start | bytes 589832 | tf_op jit(solution)/shard_map/ppermute | solution.py:520
  111.7 8.4 %collective-permute-start.13 = (bf16[3,256,128]{2,1,0:T(8,128)(2,1)S(1)}, bf16[3,256,128]{2,1,0:T(8,128)(2,1)S(1)}, u32[]{:S(2)}, u32[]{:S(2)}) collective-permute-start(bf16[3,256,128]{2,1,0:T(8,128)(2,1)S(1)} %add_convert_fusion.refs_1_), channel_id=1, source_target_pairs={{0,96},{32,0},{64,32},{96,64},{1,97},{33,1},{65,33},{97,65},{2,98}... | collective-permute-start | bytes 589832 | tf_op jit(solution)/shard_map/ppermute | solution.py:520
  112.4 7.7 %collective-permute-start.16 = (bf16[3,256,128]{2,1,0:T(8,128)(2,1)S(1)}, bf16[3,256,128]{2,1,0:T(8,128)(2,1)S(1)}, u32[]{:S(2)}, u32[]{:S(2)}) collective-permute-start(bf16[3,256,128]{2,1,0:T(8,128)(2,1)S(1)} %add_convert_fusion.refs_1_), channel_id=1, source_target_pairs={{0,1},{1,0},{2,3},{3,2},{4,5},{5,4},{6,7},{7,6},{8,9},{9,8},{10,11... | collective-permute-start | bytes 589832 | tf_op jit(solution)/shard_map/ppermute | solution.py:503
  135.4 14.1 %collective-permute-start.20 = (bf16[3,256,512]{2,1,0:T(8,128)(2,1)}, bf16[3,256,512]{2,1,0:T(8,128)(2,1)S(1)}, u32[]{:S(2)}, u32[]{:S(2)}) collective-permute-start(bf16[3,256,512]{2,1,0:T(8,128)(2,1)} %get-tuple-element.45.refs_0_), channel_id=1, source_target_pairs={{0,8},{8,16},{17,25},{25,1},{2,10},{10,18},{19,27},{27,3},{4,12},{... | collective-permute-start | bytes 2359304 | tf_op jit(solution)/shard_map/ppermute | solution.py:553
  136.7 14.7 %collective-permute-start.23 = (bf16[3,256,512]{2,1,0:T(8,128)(2,1)}, bf16[3,256,512]{2,1,0:T(8,128)(2,1)S(1)}, u32[]{:S(2)}, u32[]{:S(2)}) collective-permute-start(bf16[3,256,512]{2,1,0:T(8,128)(2,1)} %get-tuple-element.46.refs_1_), channel_id=1, source_target_pairs={{0,24},{8,0},{17,9},{25,17},{2,26},{10,2},{19,11},{27,19},{4,28},{... | collective-permute-start | bytes 2359304 | tf_op jit(solution)/shard_map/ppermute | solution.py:553
  137.4 36.7 %collective-permute-start.25 = (bf16[3,256,512]{2,1,0:T(8,128)(2,1)}, bf16[3,256,512]{2,1,0:T(8,128)(2,1)S(1)}, u32[]{:S(2)}, u32[]{:S(2)}) collective-permute-start(bf16[3,256,512]{2,1,0:T(8,128)(2,1)} %get-tuple-element.45.refs_0_), channel_id=1, source_target_pairs={{0,24},{8,0},{17,9},{25,17},{2,26},{10,2},{19,11},{27,19},{4,28},{... | collective-permute-start | bytes 2359304 | tf_op jit(solution)/shard_map/ppermute | solution.py:556
  138.1 36.0 %collective-permute-start.21 = (bf16[3,256,512]{2,1,0:T(8,128)(2,1)}, bf16[3,256,512]{2,1,0:T(8,128)(2,1)S(1)}, u32[]{:S(2)}, u32[]{:S(2)}) collective-permute-start(bf16[3,256,512]{2,1,0:T(8,128)(2,1)} %get-tuple-element.46.refs_1_), channel_id=1, source_target_pairs={{0,8},{8,16},{17,25},{25,1},{2,10},{10,18},{19,27},{27,3},{4,12},{... | collective-permute-start | bytes 2359304 | tf_op jit(solution)/shard_map/ppermute | solution.py:554
  149.5 24.6 %collective-permute-start.22 = (bf16[3,256,512]{2,1,0:T(8,128)(2,1)S(1)}, bf16[3,256,512]{2,1,0:T(8,128)(2,1)S(1)}, u32[]{:S(2)}, u32[]{:S(2)}) collective-permute-start(bf16[3,256,512]{2,1,0:T(8,128)(2,1)S(1)} %collective-permute-done.20.refs_2_), channel_id=1, source_target_pairs={{8,16},{16,24},{25,1},{1,9},{10,18},{18,26},{27,3},{3,11},{12,20},... | collective-permute-start | bytes 2359304 | tf_op jit(solution)/shard_map/ppermute | solution.py:555
  151.4 22.7 %collective-permute-start.24 = (bf16[3,256,512]{2,1,0:T(8,128)(2,1)S(1)}, bf16[3,256,512]{2,1,0:T(8,128)(2,1)S(1)}, u32[]{:S(2)}, u32[]{:S(2)}) collective-permute-start(bf16[3,256,512]{2,1,0:T(8,128)(2,1)S(1)} %collective-permute-done.23.refs_7_), channel_id=1, source_target_pairs={{24,16},{0,24},{9,1},{17,9},{26,18},{2,26},{11,3},{19,11},{28,20},... | collective-permute-start | bytes 2359304 | tf_op jit(solution)/shard_map/ppermute | solution.py:555
  (29 other events, 138.1 us)

commit v2 on v1

--- a/solution.py
+++ b/solution.py
@@ -121,11 +121,11 @@
         gate = dot(key, wb[0], ((1,), (0,)))
         up = dot(key, wb[1], ((1,), (0,)))
         dhid = dot(dout, wb[2], ((1,), (0,)))
-        sigma = jax.nn.sigmoid(gate)
+        sigma = 0.5 * jnp.tanh(0.5 * gate) + 0.5
         active = gate * sigma
         hidden = (active * up).astype(bf16)
         d_up = (dhid * active).astype(bf16)
-        d_gate = (dhid * up * sigma * (1.0 + gate * (1.0 - sigma))).astype(bf16)
+        d_gate = (dhid * up * (sigma + active * (1.0 - sigma))).astype(bf16)
         for index, (left, right) in enumerate(((key, d_gate), (key, d_up), (dout, hidden))):
             acc_ref[index] += dot(left, right, ((0,), (0,)))
         return carry
@@ -273,7 +273,7 @@
         turn_kernel,
         out_shape=[BOTH, jax.ShapeDtypeStruct((3, 8, DH, LANE), f32)]
         + [jax.ShapeDtypeStruct((3, DH, LANE), bf16)] * 4,
-        in_specs=[SSPEC] + [HBMSPEC] * 3 + [VSPEC, HBMSPEC],
+        in_specs=[SSPEC] + [ANYSPEC] * 2 + [HBMSPEC, VSPEC, HBMSPEC],
         out_specs=[HBMSPEC] * 2 + [VSPEC] * 4,
         scratch_shapes=NS_SCRATCH + GRAD_SCRATCH + [pltpu.SemaphoreType.DMA((2,))] + GRAD_PIECES,
         compiler_params=params(56),
@@ -288,7 +288,7 @@
         query = queries[rows, :]
         gate = dot(query, weights[0], ((1,), (0,)))
         up = dot(query, weights[1], ((1,), (0,)))
-        hidden = (gate * jax.nn.sigmoid(gate) * up).astype(bf16)
+        hidden = (gate * (0.5 * jnp.tanh(0.5 * gate) + 0.5) * up).astype(bf16)
         part = dot(hidden, weights[2], ((1,), (1,)))
         if half:
             out_ref[rows, column : column + DH] = (acc_ref[rows, :] + part).astype(bf16)
@@ -331,14 +331,17 @@
 
 def close_kernel(*refs):
     place_ref, g_refs, w_ref, step_ref, rest_ref = refs[0], refs[1:9], *refs[9:12]
-    one_ref, two_ref, out_ref = refs[-13:-10]
-    ns_scratch, pieces, (acc_ref, queries, q_sem), sem = refs[-10:-6], refs[-6:-4], refs[-4:-1], refs[-1]
+    both_ref, quarter_ref, out_ref = refs[-14:-11]
+    ns_scratch, pieces, (acc_ref, queries, q_sem), (quarter, sem) = refs[-11:-7], refs[-7:-5], refs[-5:-2], refs[-2:]
     both = ns_scratch[2]
     fetch = pltpu.make_async_copy(rest_ref.at[:, pl.ds(5 * DH, DH)], queries, q_sem)
     ns_body(load_pieces(g_refs, *pieces, place_ref[1]), w_ref, step_ref, ns_scratch, [fetch], False)
+    cols = pl.ds(pl.multiple_of(place_ref[1] * LANE, LANE), LANE)
+    for half in range(2):
+        quarter[half] = both[half, :, :, cols]
     done = [
-        pltpu.make_async_copy(both.at[0], one_ref, sem.at[0]),
-        pltpu.make_async_copy(both.at[1], two_ref, sem.at[1]),
+        pltpu.make_async_copy(quarter, quarter_ref, sem.at[0]),
+        pltpu.make_async_copy(both, both_ref, sem.at[1]),
     ]
     for copy in done:
         copy.start()
@@ -352,10 +355,17 @@
 def close(place, chunks, weight, step, rest, *earlier):
     return pl.pallas_call(
         close_kernel,
-        out_shape=[jax.ShapeDtypeStruct((3, DH, HALF), bf16)] * 2 + [jax.ShapeDtypeStruct((TOK, DH), bf16)],
-        in_specs=[SSPEC] + [HBMSPEC] * 9 + [VSPEC, HBMSPEC] + [ANYSPEC] * len(earlier),
+        out_shape=[
+            BOTH,
+            jax.ShapeDtypeStruct((2, 3, DH, LANE), bf16),
+            jax.ShapeDtypeStruct((TOK, DH), bf16),
+        ],
+        in_specs=[SSPEC] + [ANYSPEC] * 8 + [HBMSPEC, VSPEC, HBMSPEC] + [ANYSPEC] * len(earlier),
         out_specs=[HBMSPEC, HBMSPEC, VSPEC],
-        scratch_shapes=NS_SCRATCH + GRAD_PIECES + QUERY_SCRATCH + [pltpu.SemaphoreType.DMA((2,))],
+        scratch_shapes=NS_SCRATCH
+        + GRAD_PIECES
+        + QUERY_SCRATCH
+        + [pltpu.VMEM((2, 3, DH, LANE), bf16), pltpu.SemaphoreType.DMA((2,))],
         compiler_params=params(56),
         name="close",
         cost_estimate=cost(NS_FLOPS + 6 * TOK * DH * FF, 10 * MIB, TOK * FF),
@@ -426,30 +436,35 @@
 
 
 def final_kernel(place_ref, *refs):
-    near, sent, outs, result_ref = refs[:8], refs[8:10], refs[10:13], refs[13]
-    buf, wide, late, wide_late, in_sem, out_sem, late_sem, result_sem = refs[14:]
-    core, row = place_ref[0], place_ref[4]
+    near, opposite, sent, outs, result_ref = refs[:3], refs[3:7], refs[7:9], refs[9:12], refs[12]
+    buf, wide, late, wide_late, in_sem, out_sem, late_sem, result_sem = refs[13:]
+    core, deep, row = place_ref[0], place_ref[1], place_ref[4]
     slots = [(head, half) for head in range(2) for half in range(2)]
     fetches = [pltpu.make_async_copy(sent[i], late.at[i], late_sem.at[i]) for i in range(GROUPS)]
     for fetch in fetches:
         fetch.start()
 
-    def start(ref, slot):
-        pltpu.make_async_copy(ref, buf.at[slot], in_sem.at[slot]).start()
+    def straight(ref, slot, flip):
+        pltpu.make_async_copy(ref.at[flip], buf.at[slot], in_sem.at[slot]).start()
+
+    def pieces(slot, flip):
+        for far in range(4):
+            cols = pl.ds(pl.multiple_of(((deep + far) & 3) * LANE, LANE), LANE)
+            source = opposite[far].at[1 - flip]
+            pltpu.make_async_copy(source, buf.at[slot, :, :, cols], in_sem.at[slot]).start()
 
     for slot, (head, half) in enumerate(slots):
         away = (row - 2 * core - head) & 3
         flip = core ^ half
-        for far in range(4):
-            for side in range(2):
-                pl.when((away == far) & (flip == side))(functools.partial(start, near[2 * far + side], slot))
+        for at, far in enumerate((0, 1, 3)):
+            pl.when(away == far)(functools.partial(straight, near[at], slot, flip))
+        pl.when(away == 2)(functools.partial(pieces, slot, flip))
     done = []
     for group in range(GROUPS):
         fetches[group].wait()
         wide_late[group] = late[group].astype(f32)
         done.append(pltpu.make_async_copy(wide_late.at[group], result_ref.at[group], result_sem.at[group]))
         done[-1].start()
-
     def write(slot, carry):
         head, half = slot // 2, slot % 2
         pltpu.make_async_copy(buf.at[slot], buf.at[slot], in_sem.at[slot]).wait()
@@ -469,12 +484,12 @@
         copy.wait()
 
 
-def finish(place, near, sent):
+def finish(place, near, opposite, sent):
     return pl.pallas_call(
         final_kernel,
         out_shape=[jax.ShapeDtypeStruct((2, DH, FF), f32)] * 3
         + [jax.ShapeDtypeStruct((GROUPS, 16, 64, DH), f32)],
-        in_specs=[SSPEC] + [HBMSPEC] * 10,
+        in_specs=[SSPEC] + [ANYSPEC] * 9,
         out_specs=[HBMSPEC] * 4,
         scratch_shapes=[
             pltpu.VMEM((4, 3, DH, HALF), bf16),
@@ -486,10 +501,10 @@
             pltpu.SemaphoreType.DMA((GROUPS,)),
             pltpu.SemaphoreType.DMA((GROUPS,)),
         ],
-        compiler_params=params(56),
+        compiler_params=params(51),
         name="finish",
         cost_estimate=cost(10**6, 15 * MIB),
-    )(place, *near, *sent)
+    )(place, *near, *opposite, *sent)
 
 
 def ring(far):
@@ -522,8 +537,13 @@
     return chunks + [swap(chunk) for chunk in chunks]
 
 
-def y_pairs(start, end):
-    return [(2 * ((y + start) % 4) + y // 2, 2 * ((y + end) % 4) + y // 2) for y in range(4)]
+def y_pairs(far, across=0):
+    return [(2 * y + (y // 2 ^ across), 2 * ((y + far) % 4) + y // 2) for y in range(4)]
+
+
+def z_pairs(far):
+    cores = [2 * y + ((y + 2) % 4) // 2 for y in range(4)]
+    return [(8 * z + core, 8 * ((z + far) % 4) + core) for z in range(4) for core in cores]
 
 
 def shards(queries, keys, values, rates, step_sizes, w_gate, w_up, w_down):
@@ -548,14 +568,14 @@
 
     early = exchange(forward(rest, both, 4 * DH, partial[0]).reshape(16, 64, DH))
     chunks = gather_direct(sum_up(partial))
-    one, two, result = close(place, chunks, weights, step, rest, early)
+    both, quarter, result = close(place, chunks, weights, step, rest, early)
     move = functools.partial(lax.ppermute, axis_name=("y", "c"))
-    up, down = move(one, perm=y_pairs(0, 1)), move(two, perm=y_pairs(0, 3))
-    near = [one, two, up, move(two, perm=y_pairs(0, 1))]
-    near += [move(up, perm=y_pairs(1, 2)), move(down, perm=y_pairs(3, 2))]
-    near += [move(one, perm=y_pairs(0, 3)), down]
+    quarters = [move(quarter, perm=y_pairs(2, across=1))]
+    up, down = move(both, perm=y_pairs(1)), move(both, perm=y_pairs(3))
     late = exchange(result.reshape(16, 64, DH))
-    gate, up, down, outputs = finish(place, near, (early, late))
+    for far in (1, 2, 3):
+        quarters.append(lax.ppermute(quarters[0], ("z", "y", "c"), z_pairs(4 - far)))
+    gate, up, down, outputs = finish(place, [both, up, down], quarters, (early, late))
     return (outputs, gate, up, down)
 
 

time: 186 us -> 183 us (0.984); the launches traced: 183 us -> 182 us
  blocking collectives: 34.8 us -> 13.3 us
  starting transfers between devices: 47.7 us -> 64 us
  waiting for transfers between devices: 33 us -> 39.7 us
  Pallas kernels: 58.8 us -> 56.6 us
    all_to_all x1 -> x0, blocking collectives: 21.4 us -> none  [shards(): late = exchange(result.reshape(16, 64, DH))]
    all_to_all x0 -> x1, starting transfers between devices: none -> 8.36 us  [shards(): late = exchange(result.reshape(16, 64, DH))]
    ppermute x6, starting transfers between devices: 7.21 us -> 15.2 us  [the longest x3 9.87 us: shards(): lax.ppermute(quarters[0], ('z', 'y', 'c'), z_pairs(4 - far))]
    all_to_all x0 -> x1, waiting for transfers between devices: none -> 3.6 us  [shards(): late = exchange(result.reshape(16, 64, DH))]
    ppermute x6, waiting for transfers between devices: 10.1 us -> 13.2 us  [the longest x1 8.79 us: shards(): quarters = [move(quarter, perm=y_pairs(2, across=1))]]
    unnamed x48 -> x40, local copies, waits for them, and re-layouts: 5.08 us -> 5.29 us
  transfers between devices with their start and end apart: 29 -> 30, of which waited for: 13 -> 16; matrix products, arithmetic and copies ran while one was open for 1% -> 1% of each run, Pallas kernels for 12% -> 12%
where the time goes in v2:
time: 183 us; the launch traced here: 182 us
  starting transfers between devices  64 us (35%)
  Pallas kernels  56.6 us (31%)
  waiting for transfers between devices  39.7 us (22%)
  blocking collectives  13.3 us (7%)
  local copies, waits for them, and re-layouts  7.19 us (4%)
    pallas_call x1, Pallas kernels, turn(): pl.pallas_call(turn_kernel, out_shape=[BOTH, jax.ShapeDtypeStruct((3, 8,...  16.6 us
    pallas_call x1, Pallas kernels, close(): pl.pallas_call(close_kernel, out_shape=[BOTH, jax.ShapeDtypeStruct((2, 3,...  13.3 us
    all_gather x1, blocking collectives, gather(): whole = lax.all_gather(value, 'z')  13.3 us
    ppermute x6, starting transfers between devices, sum_up(): received = [lax.ppermute(partial[far], 'z', ring(far)) for far in (2, 1, 3)]  12.3 us
    ppermute x3, starting transfers between devices, shards(): lax.ppermute(quarters[0], ('z', 'y', 'c'), z_pairs(4 - far))  9.87 us
    ppermute x1, waiting for transfers between devices, shards(): quarters = [move(quarter, perm=y_pairs(2, across=1))]  8.79 us
    all_to_all x1, starting transfers between devices, shards(): late = exchange(result.reshape(16, 64, DH))  8.36 us
    all_to_all x1, starting transfers between devices, shards(): rest = exchange(after(second, first)).reshape(TOK, 6 * DH)  8.3 us
  transfers between devices with their start and end apart: 30, of which 16 were waited for; matrix products, arithmetic and copies ran while one was open for 1% of the time, Pallas kernels for 12%

profile of v2, /device:TPU:20, one launch (start us, length us, event | category | flops | bytes accessed | tf_op | source)
XLA Modules:
  0.0 182.1 jit_solution(13817363829685998908)
XLA Ops:
  1.3 2.7 %pack.1 = (bf16[16,64,512]{2,1,0:T(8,128)(2,1)}, bf16[16,64,512]{2,1,0:T(8,128)(2,1)}) custom-call(bf16[2,16,64,256]{3,2,1,0:T(8,128)(2,1)} %key_ref.1, bf16[2,16,64,256]{3,2,1,0:T(8,128)(2,1)} %value_ref.1, bf16[2,16,64]{2,1,0:T(8,128)(2,1)} %rate_ref.1), custom_call_target="tpu_custom_call" | custom-call | flops 1 | bytes 1 | tf_op jit(solution)/shard_map/pack/pallas_call | solution.py:60
  4.4 7.2 %all-to-all-start = ((bf16[16,64,512]{2,1,0:T(8,128)(2,1)}), bf16[16,64,512]{2,1,0:T(8,128)(2,1)S(1)}, u32[]{:S(2)}, u32[]{:S(2)}) async-start(bf16[16,64,512]{2,1,0:T(8,128)(2,1)} %get-tuple-element.28), calls=%async_computation | async-start | bytes 2097152 | tf_op jit(solution)/shard_map/all_to_all | solution.py:555
  15.5 5.8 %prepare.1 = (f32[3,8,256,128]{3,2,1,0:T(8,128)}, bf16[2,3,256,512]{3,2,1,0:T(8,128)(2,1)}, f32[8,128]{1,0:T(8,128)}) custom-call(s32[5]{0:T(128)} %stack.27.place_ref.refs_0_, f32[2,256,1024]{2,1,0:T(8,128)} %refs_0_.1, f32[2,256,1024]{2,1,0:T(8,128)} %refs_1_.1, f32[2,256,1024]{2,1,0:T(8,128)} %refs_2_.1, f32[2,256,1024]{2,1,0:T(8,128)} %copy-done.5, ...), custom_call_target="tpu_custom_call" | custom-call | flops 1 | bytes 1 | tf_op jit(solution)/shard_map/prepare/pallas_call | solution.py:418
  21.2 3.2 %join.1 = bf16[16,64,1536]{2,1,0:T(8,128)(2,1)} custom-call(bf16[16,64,512]{2,1,0:T(8,128)(2,1)} %get-tuple-element.30.own_ref, bf16[16,64,512]{2,1,0:T(8,128)(2,1)} %collective-permute-done.4.peer_ref, bf16[2,16,64,256]{3,2,1,0:T(8,128)(2,1)} %queries_ref.1, f32[8,128]{1,0:T(8,128)} %get-tuple-element.29.refs_0_.refs_4_.refs_10_), custom_call_target="tpu_custom_call" | custom-call | flops 1 | bytes 1 | tf_op jit(solution)/shard_map/join/pallas_call | solution.py:83
  25.9 8.3 %all-to-all-start.1 = ((bf16[16,64,1536]{2,1,0:T(8,128)(2,1)}), bf16[16,64,1536]{2,1,0:T(8,128)(2,1)}, u32[]{:S(2)}, u32[]{:S(2)}) async-start(bf16[16,64,1536]{2,1,0:T(8,128)(2,1)} %join.1), calls=%async_computation.1 | async-start | bytes 6291456 | tf_op jit(solution)/shard_map/all_to_all | solution.py:564
  34.2 2.7 %collective-permute-done.5.peer_ref = bf16[1024,512]{1,0:T(8,128)(2,1)S(1)} collective-permute-done((bf16[1024,512]{1,0:T(8,128)(2,1)S(1)}, bf16[1024,512]{1,0:T(8,128)(2,1)S(1)}, u32[]{:S(2)}, u32[]{:S(2)}) %collective-permute-start.5) | collective-permute-done | bytes 1048608 | tf_op jit(solution)/shard_map/ppermute | solution.py:518
  38.3 6.1 %grads.1 = (bf16[3,256,128]{2,1,0:T(8,128)(2,1)S(1)}, bf16[3,256,128]{2,1,0:T(8,128)(2,1)S(1)}, bf16[3,256,128]{2,1,0:T(8,128)(2,1)S(1)}, bf16[3,256,128]{2,1,0:T(8,128)(2,1)S(1)}) custom-call(s32[5]{0:T(128)S(1)} %copy-done.2, bf16[1024,512]{1,0:T(8,128)(2,1)S(1)} %bitcast.12, bf16[1024,512]{1,0:T(8,128)(2,1)S(1)} %collective-permute-done.5.peer_ref, ...), custom_call_target="tpu_custom_call" | custom-call | flops 3221225472 | bytes 4194304 | tf_op jit(solution)/shard_map/grads/pallas_call | solution.py:152
  44.4 4.0 %collective-permute-start.6 = (bf16[3,256,128]{2,1,0:T(8,128)(2,1)S(1)}, bf16[3,256,128]{2,1,0:T(8,128)(2,1)S(1)}, u32[]{:S(2)}, u32[]{:S(2)}) collective-permute-start(bf16[3,256,128]{2,1,0:T(8,128)(2,1)S(1)} %get-tuple-element.34), channel_id=1, source_target_pairs={{0,64},{32,96},{64,0},{96,32},{1,65},{33,97},{65,1},{97,33},{2,66}... | collective-permute-start | bytes 589832 | tf_op jit(solution)/shard_map/ppermute | solution.py:522
  51.6 2.4 %collective-permute-done.6 = bf16[3,256,128]{2,1,0:T(8,128)(2,1)S(1)} collective-permute-done((bf16[3,256,128]{2,1,0:T(8,128)(2,1)S(1)}, bf16[3,256,128]{2,1,0:T(8,128)(2,1)S(1)}, u32[]{:S(2)}, u32[]{:S(2)}) %collective-permute-start.6) | collective-permute-done | bytes 196640 | tf_op jit(solution)/shard_map/ppermute | solution.py:522
  54.0 3.7 %collective-permute-done.7 = bf16[3,256,128]{2,1,0:T(8,128)(2,1)S(1)} collective-permute-done((bf16[3,256,128]{2,1,0:T(8,128)(2,1)S(1)}, bf16[3,256,128]{2,1,0:T(8,128)(2,1)S(1)}, u32[]{:S(2)}, u32[]{:S(2)}) %collective-permute-start.7) | collective-permute-done | bytes 196640 | tf_op jit(solution)/shard_map/ppermute | solution.py:522
  58.6 13.3 %all-gather = bf16[12,256,128]{2,1,0:T(8,128)(2,1)S(1)} all-gather(bf16[3,256,128]{2,1,0:T(8,128)(2,1)S(1)} %add_convert_fusion.1), channel_id=2, replica_groups=mesh['z'=4,'y'=4,'x'=4,'c'=2] {'z'}, dimensions={0}, use_global_device_ids=true | all-gather | bytes 983040 | tf_op jit(solution)/shard_map/all_gather | solution.py:530
  75.1 16.6 %turn.1 = (bf16[2,3,256,512]{3,2,1,0:T(8,128)(2,1)}, f32[3,8,256,128]{3,2,1,0:T(8,128)}, bf16[3,256,128]{2,1,0:T(8,128)(2,1)}, bf16[3,256,128]{2,1,0:T(8,128)(2,...) custom-call(s32[5]{0:T(128)} %stack.27.place_ref.refs_0_, bf16[4,3,256,128]{3,2,1,0:T(8,128)(2,1)} %bitcast.14, ...), custom_call_target="tpu_custom_call" | custom-call | flops 7751225344 | bytes 14680064 | tf_op jit(solution)/shard_map/turn/pallas_call | solution.py:272
  93.3 2.9 %collective-permute-start.11 = (bf16[3,256,128]{2,1,0:T(8,128)(2,1)}, bf16[3,256,128]{2,1,0:T(8,128)(2,1)S(1)}, u32[]{:S(2)}, u32[]{:S(2)}) collective-permute-start(bf16[3,256,128]{2,1,0:T(8,128)(2,1)} %get-tuple-element.41), channel_id=1, source_target_pairs={{0,32},{32,64},{64,96},{96,0},{1,33},{33,65},{65,97},{97,1},{2,34}... | collective-permute-start | bytes 589832 | tf_op jit(solution)/shard_map/ppermute | solution.py:522
  96.8 4.4 %forward.1 = bf16[1024,256]{1,0:T(8,128)(2,1)} custom-call(bf16[1024,1536]{1,0:T(8,128)(2,1)} %bitcast.8.refs_5_.rest_ref.refs_11_, bf16[2,3,256,512]{3,2,1,0:T(8,128)(2,1)} %get-tuple-element.44.both_ref, bf16[3,256,128]{2,1,0:T(8,128)(2,1)} %get-tuple-element.39.refs_0_), custom_call_target="tpu_custom_call" | custom-call | flops 1610612736 | bytes 3145728 | tf_op jit(solution)/shard_map/forward/pallas_call | solution.py:320
  101.2 7.2 %all-to-all-start.2 = ((bf16[16,64,256]{2,1,0:T(8,128)(2,1)}), bf16[16,64,256]{2,1,0:T(8,128)(2,1)S(1)}, u32[]{:S(2)}, u32[]{:S(2)}) async-start(bf16[16,64,256]{2,1,0:T(8,128)(2,1)} %bitcast.15), calls=%async_computation.2 | async-start | bytes 1048576 | tf_op jit(solution)/shard_map/all_to_all | solution.py:569
  112.9 5.2 %collective-permute-done.15.refs_4_ = bf16[3,256,128]{2,1,0:T(8,128)(2,1)S(1)} collective-permute-done((bf16[3,256,128]{2,1,0:T(8,128)(2,1)S(1)}, bf16[3,256,128]{2,1,0:T(8,128)(2,1)S(1)}, u32[]{:S(2)}, u32[]{:S(2)}) %collective-permute-start.15) | collective-permute-done | bytes 196640 | tf_op jit(solution)/shard_map/ppermute | solution.py:535
  122.6 13.3 %close.1 = (bf16[2,3,256,512]{3,2,1,0:T(8,128)(2,1)}, bf16[2,3,256,128]{3,2,1,0:T(8,128)(2,1)}, bf16[1024,256]{1,0:T(8,128)(2,1)}) custom-call(s32[5]{0:T(128)} %stack.27.place_ref.refs_0_, bf16[3,256,128]{2,1,0:T(8,128)(2,1)} %copy-done.7, bf16[3,256,128]{2,1,0:T(8,128)(2,1)} %copy-done.14, bf16[3,256,128]{2,1,0:T(8,128)(2,1)} %copy-done.13, ...), custom_call_target="tpu_custom_call" | custom-call | flops 6140612608 | bytes 10485760 | tf_op jit(solution)/shard_map/close/pallas_call | solution.py:356
  141.3 8.4 %all-to-all-start.3 = ((bf16[16,64,256]{2,1,0:T(8,128)(2,1)}), bf16[16,64,256]{2,1,0:T(8,128)(2,1)S(1)}, u32[]{:S(2)}, u32[]{:S(2)}) async-start(bf16[16,64,256]{2,1,0:T(8,128)(2,1)} %bitcast.16), calls=%async_computation.3 | async-start | bytes 1048576 | tf_op jit(solution)/shard_map/all_to_all | solution.py:575
  149.7 8.8 %collective-permute-done.22.refs_3_ = bf16[2,3,256,128]{3,2,1,0:T(8,128)(2,1)S(1)} collective-permute-done((bf16[2,3,256,128]{3,2,1,0:T(8,128)(2,1)}, bf16[2,3,256,128]{3,2,1,0:T(8,128)(2,1)S(1)}, u32[]{:S(2)}, u32[]{:S(2)}) %collective-permute-start.22) | collective-permute-done | bytes 393248 | tf_op jit(solution)/shard_map/ppermute | solution.py:573
  158.5 2.8 %collective-permute-start.25 = (bf16[2,3,256,128]{3,2,1,0:T(8,128)(2,1)S(1)}, bf16[2,3,256,128]{3,2,1,0:T(8,128)(2,1)S(1)}, u32[]{:S(2)}, u32[]{:S(2)}) collective-permute-start(bf16[2,3,256,128]{3,2,1,0:T(8,128)(2,1)S(1)} %collective-permute-done.22.refs_3_), channel_id=1, source_target_pairs={{1,33},{9,41},{16,48},{24,56},{33,65},{41,73},{48,80},{56,88},{65,... | collective-permute-start | bytes 1179656 | tf_op jit(solution)/shard_map/ppermute | solution.py:577
  161.3 5.1 %collective-permute-start.24 = (bf16[2,3,256,128]{3,2,1,0:T(8,128)(2,1)S(1)}, bf16[2,3,256,128]{3,2,1,0:T(8,128)(2,1)S(1)}, u32[]{:S(2)}, u32[]{:S(2)}) collective-permute-start(bf16[2,3,256,128]{3,2,1,0:T(8,128)(2,1)S(1)} %collective-permute-done.22.refs_3_), channel_id=1, source_target_pairs={{1,65},{9,73},{16,80},{24,88},{33,97},{41,105},{48,112},{56,120},{... | collective-permute-start | bytes 1179656 | tf_op jit(solution)/shard_map/ppermute | solution.py:577
  168.3 3.6 %all-to-all-done.3.refs_8_ = bf16[16,64,256]{2,1,0:T(8,128)(2,1)S(1)} async-done(((bf16[16,64,256]{2,1,0:T(8,128)(2,1)}), bf16[16,64,256]{2,1,0:T(8,128)(2,1)S(1)}, u32[]{:S(2)}, u32[]{:S(2)}) %all-to-all-start.3) | async-done | bytes 524320 | tf_op jit(solution)/shard_map/all_to_all | solution.py:575
  172.0 2.5 %collective-permute-done.24.refs_5_ = bf16[2,3,256,128]{3,2,1,0:T(8,128)(2,1)S(1)} collective-permute-done((bf16[2,3,256,128]{3,2,1,0:T(8,128)(2,1)S(1)}, bf16[2,3,256,128]{3,2,1,0:T(8,128)(2,1)S(1)}, u32[]{:S(2)}, u32[]{:S(2)}) %collective-permute-start.24) | collective-permute-done | bytes 393248 | tf_op jit(solution)/shard_map/ppermute | solution.py:577
  177.4 4.5 %finish.1 = (f32[2,256,1024]{2,1,0:T(8,128)}, f32[2,256,1024]{2,1,0:T(8,128)}, f32[2,256,1024]{2,1,0:T(8,128)}, f32[2,16,64,256]{3,2,1,0:T(8,128)}) custom-call(s32[5]{0:T(128)S(1)} %copy-done.3, bf16[2,3,256,512]{3,2,1,0:T(8,128)(2,1)} %get-tuple-element.45.refs_0_, bf16[2,3,256,512]{3,2,1,0:T(8,128)(2,1)} %collective-permute-done.20.refs_1_, ...), custom_call_target="tpu_custom_call" | custom-call | flops 1000000 | bytes 15728640 | tf_op jit(solution)/shard_map/finish/pallas_call | solution.py:488
  (90 shorter events, 36.3 us)
Async XLA Ops:
  0.6 13.5 %collective-permute-start = (f32[2,256,1024]{2,1,0:T(8,128)}, f32[2,256,1024]{2,1,0:T(8,128)S(1)}, u32[]{:S(2)}, u32[]{:S(2)}) collective-permute-start(f32[2,256,1024]{2,1,0:T(8,128)} %refs_0_.1), channel_id=1, source_target_pairs={{0,1},{1,0},{2,3},{3,2},{4,5},{5,4},{6,7},{7,6},{8,9},{9,8},{10,11... | collective-permute-start | bytes 6291464 | tf_op jit(solution)/shard_map/ppermute | solution.py:518
  0.7 13.4 %collective-permute-start.1 = (f32[2,256,1024]{2,1,0:T(8,128)}, f32[2,256,1024]{2,1,0:T(8,128)}, u32[]{:S(2)}, u32[]{:S(2)}) collective-permute-start(f32[2,256,1024]{2,1,0:T(8,128)} %refs_1_.1), channel_id=1, source_target_pairs={{0,1},{1,0},{2,3},{3,2},{4,5},{5,4},{6,7},{7,6},{8,9},{9,8},{10,11... | collective-permute-start | bytes 6291464 | tf_op jit(solution)/shard_map/ppermute | solution.py:518
  1.2 12.9 %collective-permute-start.2 = (f32[2,256,1024]{2,1,0:T(8,128)}, f32[2,256,1024]{2,1,0:T(8,128)}, u32[]{:S(2)}, u32[]{:S(2)}) collective-permute-start(f32[2,256,1024]{2,1,0:T(8,128)} %refs_2_.1), channel_id=1, source_target_pairs={{0,1},{1,0},{2,3},{3,2},{4,5},{5,4},{6,7},{7,6},{8,9},{9,8},{10,11... | collective-permute-start | bytes 6291464 | tf_op jit(solution)/shard_map/ppermute | solution.py:518
  4.0 17.2 %collective-permute-start.4 = (bf16[16,64,512]{2,1,0:T(8,128)(2,1)}, bf16[16,64,512]{2,1,0:T(8,128)(2,1)}, u32[]{:S(2)}, u32[]{:S(2)}) collective-permute-start(bf16[16,64,512]{2,1,0:T(8,128)(2,1)} %get-tuple-element.30.own_ref), channel_id=1, source_target_pairs={{0,1},{1,0},{2,3},{3,2},{4,5},{5,4},{6,7},{7,6},{8,9},{9,8},{10,11... | collective-permute-start | bytes 3145736 | tf_op jit(solution)/shard_map/ppermute | solution.py:518
  4.4 21.5 %all-to-all-start = ((bf16[16,64,512]{2,1,0:T(8,128)(2,1)}), bf16[16,64,512]{2,1,0:T(8,128)(2,1)S(1)}, u32[]{:S(2)}, u32[]{:S(2)}) async-start(bf16[16,64,512]{2,1,0:T(8,128)(2,1)} %get-tuple-element.28), calls=%async_computation | async-start | bytes 2097152 | tf_op jit(solution)/shard_map/all_to_all | solution.py:555
  25.9 48.3 %all-to-all-start.1 = ((bf16[16,64,1536]{2,1,0:T(8,128)(2,1)}), bf16[16,64,1536]{2,1,0:T(8,128)(2,1)}, u32[]{:S(2)}, u32[]{:S(2)}) async-start(bf16[16,64,1536]{2,1,0:T(8,128)(2,1)} %join.1), calls=%async_computation.1 | async-start | bytes 6291456 | tf_op jit(solution)/shard_map/all_to_all | solution.py:564
  44.4 9.6 %collective-permute-start.6 = (bf16[3,256,128]{2,1,0:T(8,128)(2,1)S(1)}, bf16[3,256,128]{2,1,0:T(8,128)(2,1)S(1)}, u32[]{:S(2)}, u32[]{:S(2)}) collective-permute-start(bf16[3,256,128]{2,1,0:T(8,128)(2,1)S(1)} %get-tuple-element.34), channel_id=1, source_target_pairs={{0,64},{32,96},{64,0},{96,32},{1,65},{33,97},{65,1},{97,33},{2,66}... | collective-permute-start | bytes 589832 | tf_op jit(solution)/shard_map/ppermute | solution.py:522
  48.3 9.4 %collective-permute-start.7 = (bf16[3,256,128]{2,1,0:T(8,128)(2,1)S(1)}, bf16[3,256,128]{2,1,0:T(8,128)(2,1)S(1)}, u32[]{:S(2)}, u32[]{:S(2)}) collective-permute-start(bf16[3,256,128]{2,1,0:T(8,128)(2,1)S(1)} %get-tuple-element.35), channel_id=1, source_target_pairs={{0,32},{32,64},{64,96},{96,0},{1,33},{33,65},{65,97},{97,1},{2,34}... | collective-permute-start | bytes 589832 | tf_op jit(solution)/shard_map/ppermute | solution.py:522
  49.3 9.1 %collective-permute-start.8 = (bf16[3,256,128]{2,1,0:T(8,128)(2,1)S(1)}, bf16[3,256,128]{2,1,0:T(8,128)(2,1)S(1)}, u32[]{:S(2)}, u32[]{:S(2)}) collective-permute-start(bf16[3,256,128]{2,1,0:T(8,128)(2,1)S(1)} %get-tuple-element.36), channel_id=1, source_target_pairs={{0,96},{32,0},{64,32},{96,64},{1,97},{33,1},{65,33},{97,65},{2,98}... | collective-permute-start | bytes 589832 | tf_op jit(solution)/shard_map/ppermute | solution.py:522
  91.7 16.7 %collective-permute-start.10 = (bf16[3,256,128]{2,1,0:T(8,128)(2,1)}, bf16[3,256,128]{2,1,0:T(8,128)(2,1)S(1)}, u32[]{:S(2)}, u32[]{:S(2)}) collective-permute-start(bf16[3,256,128]{2,1,0:T(8,128)(2,1)} %get-tuple-element.40), channel_id=1, source_target_pairs={{0,64},{32,96},{64,0},{96,32},{1,65},{33,97},{65,1},{97,33},{2,66}... | collective-permute-start | bytes 589832 | tf_op jit(solution)/shard_map/ppermute | solution.py:522
  93.3 15.2 %collective-permute-start.11 = (bf16[3,256,128]{2,1,0:T(8,128)(2,1)}, bf16[3,256,128]{2,1,0:T(8,128)(2,1)S(1)}, u32[]{:S(2)}, u32[]{:S(2)}) collective-permute-start(bf16[3,256,128]{2,1,0:T(8,128)(2,1)} %get-tuple-element.41), channel_id=1, source_target_pairs={{0,32},{32,64},{64,96},{96,0},{1,33},{33,65},{65,97},{97,1},{2,34}... | collective-permute-start | bytes 589832 | tf_op jit(solution)/shard_map/ppermute | solution.py:522
  96.2 12.3 %collective-permute-start.12 = (bf16[3,256,128]{2,1,0:T(8,128)(2,1)}, bf16[3,256,128]{2,1,0:T(8,128)(2,1)S(1)}, u32[]{:S(2)}, u32[]{:S(2)}) collective-permute-start(bf16[3,256,128]{2,1,0:T(8,128)(2,1)} %get-tuple-element.42), channel_id=1, source_target_pairs={{0,96},{32,0},{64,32},{96,64},{1,97},{33,1},{65,33},{97,65},{2,98}... | collective-permute-start | bytes 589832 | tf_op jit(solution)/shard_map/ppermute | solution.py:522
  101.2 19.3 %all-to-all-start.2 = ((bf16[16,64,256]{2,1,0:T(8,128)(2,1)}), bf16[16,64,256]{2,1,0:T(8,128)(2,1)S(1)}, u32[]{:S(2)}, u32[]{:S(2)}) async-start(bf16[16,64,256]{2,1,0:T(8,128)(2,1)} %bitcast.15), calls=%async_computation.2 | async-start | bytes 1048576 | tf_op jit(solution)/shard_map/all_to_all | solution.py:569
  108.6 9.5 %collective-permute-start.15 = (bf16[3,256,128]{2,1,0:T(8,128)(2,1)S(1)}, bf16[3,256,128]{2,1,0:T(8,128)(2,1)S(1)}, u32[]{:S(2)}, u32[]{:S(2)}) collective-permute-start(bf16[3,256,128]{2,1,0:T(8,128)(2,1)S(1)} %add_convert_fusion.refs_1_), channel_id=1, source_target_pairs={{0,32},{32,64},{64,96},{96,0},{1,33},{33,65},{65,97},{97,1},{2,34}... | collective-permute-start | bytes 589832 | tf_op jit(solution)/shard_map/ppermute | solution.py:535
  110.1 9.8 %collective-permute-start.14 = (bf16[3,256,128]{2,1,0:T(8,128)(2,1)S(1)}, bf16[3,256,128]{2,1,0:T(8,128)(2,1)S(1)}, u32[]{:S(2)}, u32[]{:S(2)}) collective-permute-start(bf16[3,256,128]{2,1,0:T(8,128)(2,1)S(1)} %add_convert_fusion.refs_1_), channel_id=1, source_target_pairs={{0,64},{32,96},{64,0},{96,32},{1,65},{33,97},{65,1},{97,33},{2,66}... | collective-permute-start | bytes 589832 | tf_op jit(solution)/shard_map/ppermute | solution.py:535
  112.2 8.4 %collective-permute-start.13 = (bf16[3,256,128]{2,1,0:T(8,128)(2,1)S(1)}, bf16[3,256,128]{2,1,0:T(8,128)(2,1)S(1)}, u32[]{:S(2)}, u32[]{:S(2)}) collective-permute-start(bf16[3,256,128]{2,1,0:T(8,128)(2,1)S(1)} %add_convert_fusion.refs_1_), channel_id=1, source_target_pairs={{0,96},{32,0},{64,32},{96,64},{1,97},{33,1},{65,33},{97,65},{2,98}... | collective-permute-start | bytes 589832 | tf_op jit(solution)/shard_map/ppermute | solution.py:535
  112.9 7.7 %collective-permute-start.16 = (bf16[3,256,128]{2,1,0:T(8,128)(2,1)S(1)}, bf16[3,256,128]{2,1,0:T(8,128)(2,1)S(1)}, u32[]{:S(2)}, u32[]{:S(2)}) collective-permute-start(bf16[3,256,128]{2,1,0:T(8,128)(2,1)S(1)} %add_convert_fusion.refs_1_), channel_id=1, source_target_pairs={{0,1},{1,0},{2,3},{3,2},{4,5},{5,4},{6,7},{7,6},{8,9},{9,8},{10,11... | collective-permute-start | bytes 589832 | tf_op jit(solution)/shard_map/ppermute | solution.py:518
  136.0 40.3 %collective-permute-start.21 = (bf16[2,3,256,512]{3,2,1,0:T(8,128)(2,1)}, bf16[2,3,256,512]{3,2,1,0:T(8,128)(2,1)}, u32[]{:S(2)}, u32[]{:S(2)}) collective-permute-start(bf16[2,3,256,512]{3,2,1,0:T(8,128)(2,1)} %get-tuple-element.45.refs_0_), channel_id=1, source_target_pairs={{0,24},{8,0},{17,9},{25,17},{2,26},{10,2},{19,11},{27,19},{4,28},{... | collective-permute-start | bytes 4718600 | tf_op jit(solution)/shard_map/ppermute | solution.py:574
  137.8 38.5 %collective-permute-start.20 = (bf16[2,3,256,512]{3,2,1,0:T(8,128)(2,1)}, bf16[2,3,256,512]{3,2,1,0:T(8,128)(2,1)}, u32[]{:S(2)}, u32[]{:S(2)}) collective-permute-start(bf16[2,3,256,512]{3,2,1,0:T(8,128)(2,1)} %get-tuple-element.45.refs_0_), channel_id=1, source_target_pairs={{0,8},{8,16},{17,25},{25,1},{2,10},{10,18},{19,27},{27,3},{4,12},{... | collective-permute-start | bytes 4718600 | tf_op jit(solution)/shard_map/ppermute | solution.py:574
  139.1 19.4 %collective-permute-start.22 = (bf16[2,3,256,128]{3,2,1,0:T(8,128)(2,1)}, bf16[2,3,256,128]{3,2,1,0:T(8,128)(2,1)S(1)}, u32[]{:S(2)}, u32[]{:S(2)}) collective-permute-start(bf16[2,3,256,128]{3,2,1,0:T(8,128)(2,1)} %get-tuple-element.46), channel_id=1, source_target_pairs={{1,16},{9,24},{16,1},{24,9},{3,18},{11,26},{18,3},{26,11},{5,20},{... | collective-permute-start | bytes 1179656 | tf_op jit(solution)/shard_map/ppermute | solution.py:573
  141.3 30.6 %all-to-all-start.3 = ((bf16[16,64,256]{2,1,0:T(8,128)(2,1)}), bf16[16,64,256]{2,1,0:T(8,128)(2,1)S(1)}, u32[]{:S(2)}, u32[]{:S(2)}) async-start(bf16[16,64,256]{2,1,0:T(8,128)(2,1)} %bitcast.16), calls=%async_computation.3 | async-start | bytes 1048576 | tf_op jit(solution)/shard_map/all_to_all | solution.py:575
  158.5 13.5 %collective-permute-start.25 = (bf16[2,3,256,128]{3,2,1,0:T(8,128)(2,1)S(1)}, bf16[2,3,256,128]{3,2,1,0:T(8,128)(2,1)S(1)}, u32[]{:S(2)}, u32[]{:S(2)}) collective-permute-start(bf16[2,3,256,128]{3,2,1,0:T(8,128)(2,1)S(1)} %collective-permute-done.22.refs_3_), channel_id=1, source_target_pairs={{1,33},{9,41},{16,48},{24,56},{33,65},{41,73},{48,80},{56,88},{65,... | collective-permute-start | bytes 1179656 | tf_op jit(solution)/shard_map/ppermute | solution.py:577
  161.3 13.1 %collective-permute-start.24 = (bf16[2,3,256,128]{3,2,1,0:T(8,128)(2,1)S(1)}, bf16[2,3,256,128]{3,2,1,0:T(8,128)(2,1)S(1)}, u32[]{:S(2)}, u32[]{:S(2)}) collective-permute-start(bf16[2,3,256,128]{3,2,1,0:T(8,128)(2,1)S(1)} %collective-permute-done.22.refs_3_), channel_id=1, source_target_pairs={{1,65},{9,73},{16,80},{24,88},{33,97},{41,105},{48,112},{56,120},{... | collective-permute-start | bytes 1179656 | tf_op jit(solution)/shard_map/ppermute | solution.py:577
  166.4 9.9 %collective-permute-start.23 = (bf16[2,3,256,128]{3,2,1,0:T(8,128)(2,1)S(1)}, bf16[2,3,256,128]{3,2,1,0:T(8,128)(2,1)S(1)}, u32[]{:S(2)}, u32[]{:S(2)}) collective-permute-start(bf16[2,3,256,128]{3,2,1,0:T(8,128)(2,1)S(1)} %collective-permute-done.22.refs_3_), channel_id=1, source_target_pairs={{1,97},{9,105},{16,112},{24,120},{33,1},{41,9},{48,16},{56,24},{65... | collective-permute-start | bytes 1179656 | tf_op jit(solution)/shard_map/ppermute | solution.py:577
  (26 other events, 134.3 us)

commit v3 on v2

--- a/solution.py
+++ b/solution.py
@@ -155,7 +155,7 @@
         in_specs=[SSPEC] + [HBMSPEC] * 3,
         out_specs=[VSPEC] * 4,
         scratch_shapes=GRAD_SCRATCH + [pltpu.VMEM((3, DH, HALF), bf16), pltpu.SemaphoreType.DMA(())],
-        compiler_params=params(24),
+        compiler_params=params(50),
         name="grads",
         cost_estimate=cost(12 * 2 * TOK * DH * HALF, 4 * MIB, 2 * TOK * HALF),
     )(place, own, peer, both)
@@ -330,19 +330,28 @@
 
 
 def close_kernel(*refs):
-    place_ref, g_refs, w_ref, step_ref, rest_ref = refs[0], refs[1:9], *refs[9:12]
-    both_ref, quarter_ref, out_ref = refs[-14:-11]
-    ns_scratch, pieces, (acc_ref, queries, q_sem), (quarter, sem) = refs[-11:-7], refs[-7:-5], refs[-5:-2], refs[-2:]
+    place_ref, g_refs, w_ref, step_ref, rest_ref, early_ref = refs[0], refs[1:9], *refs[9:13]
+    both_ref, quarter_ref, out_ref, outputs_ref = refs[13:17]
+    ns_scratch, pieces, (acc_ref, queries, q_sem), (quarter, sem, narrow, wide) = (
+        refs[17:21],
+        refs[21:23],
+        refs[23:26],
+        refs[26:],
+    )
     both = ns_scratch[2]
     fetch = pltpu.make_async_copy(rest_ref.at[:, pl.ds(5 * DH, DH)], queries, q_sem)
-    ns_body(load_pieces(g_refs, *pieces, place_ref[1]), w_ref, step_ref, ns_scratch, [fetch], False)
+    early = pltpu.make_async_copy(early_ref, narrow, sem.at[2])
+    ns_body(load_pieces(g_refs, *pieces, place_ref[1]), w_ref, step_ref, ns_scratch, [fetch, early], False)
     cols = pl.ds(pl.multiple_of(place_ref[1] * LANE, LANE), LANE)
     for half in range(2):
         quarter[half] = both[half, :, :, cols]
     done = [
         pltpu.make_async_copy(quarter, quarter_ref, sem.at[0]),
         pltpu.make_async_copy(both, both_ref, sem.at[1]),
+        pltpu.make_async_copy(wide, outputs_ref.at[0], sem.at[3]),
     ]
+    early.wait()
+    wide[...] = narrow[...].astype(f32)
     for copy in done:
         copy.start()
     fetch.wait()
@@ -352,24 +361,30 @@
         copy.wait()
 
 
-def close(place, chunks, weight, step, rest, *earlier):
+def close(place, chunks, weight, step, rest, early):
     return pl.pallas_call(
         close_kernel,
         out_shape=[
             BOTH,
             jax.ShapeDtypeStruct((2, 3, DH, LANE), bf16),
             jax.ShapeDtypeStruct((TOK, DH), bf16),
+            jax.ShapeDtypeStruct((GROUPS, 16, 64, DH), f32),
         ],
-        in_specs=[SSPEC] + [ANYSPEC] * 8 + [HBMSPEC, VSPEC, HBMSPEC] + [ANYSPEC] * len(earlier),
-        out_specs=[HBMSPEC, HBMSPEC, VSPEC],
+        in_specs=[SSPEC] + [ANYSPEC] * 8 + [HBMSPEC, VSPEC, HBMSPEC, ANYSPEC],
+        out_specs=[HBMSPEC, HBMSPEC, VSPEC, HBMSPEC],
         scratch_shapes=NS_SCRATCH
         + GRAD_PIECES
         + QUERY_SCRATCH
-        + [pltpu.VMEM((2, 3, DH, LANE), bf16), pltpu.SemaphoreType.DMA((2,))],
-        compiler_params=params(56),
+        + [
+            pltpu.VMEM((2, 3, DH, LANE), bf16),
+            pltpu.SemaphoreType.DMA((4,)),
+            pltpu.VMEM((16, 64, DH), bf16),
+            pltpu.VMEM((16, 64, DH), f32),
+        ],
+        compiler_params=params(52),
         name="close",
         cost_estimate=cost(NS_FLOPS + 6 * TOK * DH * FF, 10 * MIB, TOK * FF),
-    )(place, *chunks, weight, step, rest, *earlier)
+    )(place, *chunks, weight, step, rest, early)
 
 
 def prep_kernel(place_ref, *refs):
@@ -436,13 +451,12 @@
 
 
 def final_kernel(place_ref, *refs):
-    near, opposite, sent, outs, result_ref = refs[:3], refs[3:7], refs[7:9], refs[9:12], refs[12]
+    near, opposite, late_ref, outs, result_ref = refs[:3], refs[3:7], refs[7], refs[9:12], refs[12]
     buf, wide, late, wide_late, in_sem, out_sem, late_sem, result_sem = refs[13:]
     core, deep, row = place_ref[0], place_ref[1], place_ref[4]
     slots = [(head, half) for head in range(2) for half in range(2)]
-    fetches = [pltpu.make_async_copy(sent[i], late.at[i], late_sem.at[i]) for i in range(GROUPS)]
-    for fetch in fetches:
-        fetch.start()
+    fetch = pltpu.make_async_copy(late_ref, late, late_sem)
+    fetch.start()
 
     def straight(ref, slot, flip):
         pltpu.make_async_copy(ref.at[flip], buf.at[slot], in_sem.at[slot]).start()
@@ -459,12 +473,11 @@
         for at, far in enumerate((0, 1, 3)):
             pl.when(away == far)(functools.partial(straight, near[at], slot, flip))
         pl.when(away == 2)(functools.partial(pieces, slot, flip))
-    done = []
-    for group in range(GROUPS):
-        fetches[group].wait()
-        wide_late[group] = late[group].astype(f32)
-        done.append(pltpu.make_async_copy(wide_late.at[group], result_ref.at[group], result_sem.at[group]))
-        done[-1].start()
+    fetch.wait()
+    wide_late[...] = late[...].astype(f32)
+    done = [pltpu.make_async_copy(wide_late, result_ref.at[1], result_sem)]
+    done[0].start()
+
     def write(slot, carry):
         head, half = slot // 2, slot % 2
         pltpu.make_async_copy(buf.at[slot], buf.at[slot], in_sem.at[slot]).wait()
@@ -484,27 +497,28 @@
         copy.wait()
 
 
-def finish(place, near, opposite, sent):
+def finish(place, near, opposite, late, outputs):
     return pl.pallas_call(
         final_kernel,
         out_shape=[jax.ShapeDtypeStruct((2, DH, FF), f32)] * 3
         + [jax.ShapeDtypeStruct((GROUPS, 16, 64, DH), f32)],
-        in_specs=[SSPEC] + [ANYSPEC] * 9,
+        in_specs=[SSPEC] + [ANYSPEC] * 8 + [HBMSPEC],
         out_specs=[HBMSPEC] * 4,
         scratch_shapes=[
             pltpu.VMEM((4, 3, DH, HALF), bf16),
             pltpu.VMEM((4, 3, DH, HALF), f32),
-            pltpu.VMEM((GROUPS, 16, 64, DH), bf16),
-            pltpu.VMEM((GROUPS, 16, 64, DH), f32),
+            pltpu.VMEM((16, 64, DH), bf16),
+            pltpu.VMEM((16, 64, DH), f32),
             pltpu.SemaphoreType.DMA((4,)),
             pltpu.SemaphoreType.DMA((4, 3)),
-            pltpu.SemaphoreType.DMA((GROUPS,)),
-            pltpu.SemaphoreType.DMA((GROUPS,)),
+            pltpu.SemaphoreType.DMA(()),
+            pltpu.SemaphoreType.DMA(()),
         ],
+        input_output_aliases={9: 3},
         compiler_params=params(51),
         name="finish",
         cost_estimate=cost(10**6, 15 * MIB),
-    )(place, *near, *opposite, *sent)
+    )(place, *near, *opposite, late, outputs)
 
 
 def ring(far):
@@ -568,14 +582,14 @@
 
     early = exchange(forward(rest, both, 4 * DH, partial[0]).reshape(16, 64, DH))
     chunks = gather_direct(sum_up(partial))
-    both, quarter, result = close(place, chunks, weights, step, rest, early)
+    both, quarter, result, outputs = close(place, chunks, weights, step, rest, early)
     move = functools.partial(lax.ppermute, axis_name=("y", "c"))
     quarters = [move(quarter, perm=y_pairs(2, across=1))]
     up, down = move(both, perm=y_pairs(1)), move(both, perm=y_pairs(3))
     late = exchange(result.reshape(16, 64, DH))
     for far in (1, 2, 3):
         quarters.append(lax.ppermute(quarters[0], ("z", "y", "c"), z_pairs(4 - far)))
-    gate, up, down, outputs = finish(place, [both, up, down], quarters, (early, late))
+    gate, up, down, outputs = finish(place, [both, up, down], quarters, late, outputs)
     return (outputs, gate, up, down)
 
 

time: 183 us -> 181 us (0.989)
  local copies, waits for them, and re-layouts: 7.19 us -> 4.08 us
    unnamed x40 -> x22, local copies, waits for them, and re-layouts: 5.29 us -> 2.2 us
  transfers between devices with their start and end apart: 30 -> 30, of which waited for: 16 -> 16; matrix products, arithmetic and copies ran while one was open for 1% -> 1% of each run, Pallas kernels for 12% -> 13%
where the time goes in v3:
time: 181 us
  starting transfers between devices  64 us (35%)
  Pallas kernels  58.2 us (32%)
  waiting for transfers between devices  39.7 us (22%)
  blocking collectives  13.3 us (7%)
  local copies, waits for them, and re-layouts  4.08 us (2%)
    pallas_call x1, Pallas kernels, turn(): pl.pallas_call(turn_kernel, out_shape=[BOTH, jax.ShapeDtypeStruct((3, 8,...  16.6 us
    pallas_call x1, Pallas kernels, close(): pl.pallas_call(close_kernel, out_shape=[BOTH, jax.ShapeDtypeStruct((2, 3,...  14 us
    all_gather x1, blocking collectives, gather(): whole = lax.all_gather(value, 'z')  13.3 us
    ppermute x6, starting transfers between devices, sum_up(): received = [lax.ppermute(partial[far], 'z', ring(far)) for far in (2, 1, 3)]  12.3 us
    ppermute x3, starting transfers between devices, shards(): lax.ppermute(quarters[0], ('z', 'y', 'c'), z_pairs(4 - far))  9.86 us
    ppermute x1, waiting for transfers between devices, shards(): quarters = [move(quarter, perm=y_pairs(2, across=1))]  8.69 us
    all_to_all x1, starting transfers between devices, shards(): late = exchange(result.reshape(16, 64, DH))  8.34 us
    all_to_all x1, starting transfers between devices, shards(): rest = exchange(after(second, first)).reshape(TOK, 6 * DH)  8.33 us
  transfers between devices with their start and end apart: 30, of which 16 were waited for; matrix products, arithmetic and copies ran while one was open for 1% of the time, Pallas kernels for 13%

profile of v3, /device:TPU:20, one launch (start us, length us, event | category | flops | bytes accessed | tf_op | source)
XLA Modules:
  0.0 180.5 jit_solution(2411597337222433403)
XLA Ops:
  1.3 2.7 %pack.1 = (bf16[16,64,512]{2,1,0:T(8,128)(2,1)}, bf16[16,64,512]{2,1,0:T(8,128)(2,1)}) custom-call(bf16[2,16,64,256]{3,2,1,0:T(8,128)(2,1)} %key_ref.1, bf16[2,16,64,256]{3,2,1,0:T(8,128)(2,1)} %value_ref.1, bf16[2,16,64]{2,1,0:T(8,128)(2,1)} %rate_ref.1), custom_call_target="tpu_custom_call" | custom-call | flops 1 | bytes 1 | tf_op jit(solution)/shard_map/pack/pallas_call | solution.py:60
  4.4 7.2 %all-to-all-start = ((bf16[16,64,512]{2,1,0:T(8,128)(2,1)}), bf16[16,64,512]{2,1,0:T(8,128)(2,1)S(1)}, u32[]{:S(2)}, u32[]{:S(2)}) async-start(bf16[16,64,512]{2,1,0:T(8,128)(2,1)} %get-tuple-element.29), calls=%async_computation | async-start | bytes 2097152 | tf_op jit(solution)/shard_map/all_to_all | solution.py:569
  15.5 5.7 %prepare.1 = (f32[3,8,256,128]{3,2,1,0:T(8,128)}, bf16[2,3,256,512]{3,2,1,0:T(8,128)(2,1)}, f32[8,128]{1,0:T(8,128)}) custom-call(s32[5]{0:T(128)} %stack.27.place_ref.refs_0_, f32[2,256,1024]{2,1,0:T(8,128)} %refs_0_.1, f32[2,256,1024]{2,1,0:T(8,128)} %refs_1_.1, f32[2,256,1024]{2,1,0:T(8,128)} %refs_2_.1, f32[2,256,1024]{2,1,0:T(8,128)} %copy-done.3, ...), custom_call_target="tpu_custom_call" | custom-call | flops 1 | bytes 1 | tf_op jit(solution)/shard_map/prepare/pallas_call | solution.py:433
  21.2 3.2 %join.1 = bf16[16,64,1536]{2,1,0:T(8,128)(2,1)} custom-call(bf16[16,64,512]{2,1,0:T(8,128)(2,1)} %get-tuple-element.31.own_ref, bf16[16,64,512]{2,1,0:T(8,128)(2,1)} %collective-permute-done.4.peer_ref, bf16[2,16,64,256]{3,2,1,0:T(8,128)(2,1)} %queries_ref.1, f32[8,128]{1,0:T(8,128)} %get-tuple-element.30.refs_0_.refs_4_.refs_10_), custom_call_target="tpu_custom_call" | custom-call | flops 1 | bytes 1 | tf_op jit(solution)/shard_map/join/pallas_call | solution.py:83
  25.9 8.3 %all-to-all-start.1 = ((bf16[16,64,1536]{2,1,0:T(8,128)(2,1)}), bf16[16,64,1536]{2,1,0:T(8,128)(2,1)}, u32[]{:S(2)}, u32[]{:S(2)}) async-start(bf16[16,64,1536]{2,1,0:T(8,128)(2,1)} %join.1), calls=%async_computation.1 | async-start | bytes 6291456 | tf_op jit(solution)/shard_map/all_to_all | solution.py:578
  34.2 2.7 %collective-permute-done.5.peer_ref = bf16[1024,512]{1,0:T(8,128)(2,1)S(1)} collective-permute-done((bf16[1024,512]{1,0:T(8,128)(2,1)S(1)}, bf16[1024,512]{1,0:T(8,128)(2,1)S(1)}, u32[]{:S(2)}, u32[]{:S(2)}) %collective-permute-start.5) | collective-permute-done | bytes 1048608 | tf_op jit(solution)/shard_map/ppermute | solution.py:532
  36.9 7.1 %grads.1 = (bf16[3,256,128]{2,1,0:T(8,128)(2,1)S(1)}, bf16[3,256,128]{2,1,0:T(8,128)(2,1)S(1)}, bf16[3,256,128]{2,1,0:T(8,128)(2,1)S(1)}, bf16[3,256,128]{2,1,0:T(8,128)(2,1)S(1)}) custom-call(s32[5]{0:T(128)S(1)} %copy-done, bf16[1024,512]{1,0:T(8,128)(2,1)S(1)} %bitcast.12, bf16[1024,512]{1,0:T(8,128)(2,1)S(1)} %collective-permute-done.5.peer_ref, ...), custom_call_target="tpu_custom_call" | custom-call | flops 3221225472 | bytes 4194304 | tf_op jit(solution)/shard_map/grads/pallas_call | solution.py:152
  44.0 4.0 %collective-permute-start.6 = (bf16[3,256,128]{2,1,0:T(8,128)(2,1)S(1)}, bf16[3,256,128]{2,1,0:T(8,128)(2,1)S(1)}, u32[]{:S(2)}, u32[]{:S(2)}) collective-permute-start(bf16[3,256,128]{2,1,0:T(8,128)(2,1)S(1)} %get-tuple-element.35), channel_id=1, source_target_pairs={{0,64},{32,96},{64,0},{96,32},{1,65},{33,97},{65,1},{97,33},{2,66}... | collective-permute-start | bytes 589832 | tf_op jit(solution)/shard_map/ppermute | solution.py:536
  51.2 2.4 %collective-permute-done.6 = bf16[3,256,128]{2,1,0:T(8,128)(2,1)S(1)} collective-permute-done((bf16[3,256,128]{2,1,0:T(8,128)(2,1)S(1)}, bf16[3,256,128]{2,1,0:T(8,128)(2,1)S(1)}, u32[]{:S(2)}, u32[]{:S(2)}) %collective-permute-start.6) | collective-permute-done | bytes 196640 | tf_op jit(solution)/shard_map/ppermute | solution.py:536
  53.7 3.7 %collective-permute-done.7 = bf16[3,256,128]{2,1,0:T(8,128)(2,1)S(1)} collective-permute-done((bf16[3,256,128]{2,1,0:T(8,128)(2,1)S(1)}, bf16[3,256,128]{2,1,0:T(8,128)(2,1)S(1)}, u32[]{:S(2)}, u32[]{:S(2)}) %collective-permute-start.7) | collective-permute-done | bytes 196640 | tf_op jit(solution)/shard_map/ppermute | solution.py:536
  58.2 13.3 %all-gather = bf16[12,256,128]{2,1,0:T(8,128)(2,1)S(1)} all-gather(bf16[3,256,128]{2,1,0:T(8,128)(2,1)S(1)} %add_convert_fusion.1), channel_id=2, replica_groups=mesh['z'=4,'y'=4,'x'=4,'c'=2] {'z'}, dimensions={0}, use_global_device_ids=true | all-gather | bytes 983040 | tf_op jit(solution)/shard_map/all_gather | solution.py:544
  74.7 16.6 %turn.1 = (bf16[2,3,256,512]{3,2,1,0:T(8,128)(2,1)}, f32[3,8,256,128]{3,2,1,0:T(8,128)}, bf16[3,256,128]{2,1,0:T(8,128)(2,1)}, bf16[3,256,128]{2,1,0:T(8,128)(2,...) custom-call(s32[5]{0:T(128)} %stack.27.place_ref.refs_0_, bf16[4,3,256,128]{3,2,1,0:T(8,128)(2,1)} %bitcast.14, ...), custom_call_target="tpu_custom_call" | custom-call | flops 7751225344 | bytes 14680064 | tf_op jit(solution)/shard_map/turn/pallas_call | solution.py:272
  92.9 2.9 %collective-permute-start.11 = (bf16[3,256,128]{2,1,0:T(8,128)(2,1)}, bf16[3,256,128]{2,1,0:T(8,128)(2,1)S(1)}, u32[]{:S(2)}, u32[]{:S(2)}) collective-permute-start(bf16[3,256,128]{2,1,0:T(8,128)(2,1)} %get-tuple-element.42), channel_id=1, source_target_pairs={{0,32},{32,64},{64,96},{96,0},{1,33},{33,65},{65,97},{97,1},{2,34}... | collective-permute-start | bytes 589832 | tf_op jit(solution)/shard_map/ppermute | solution.py:536
  96.4 4.4 %forward.1 = bf16[1024,256]{1,0:T(8,128)(2,1)} custom-call(bf16[1024,1536]{1,0:T(8,128)(2,1)} %bitcast.8.refs_5_.rest_ref.refs_11_, bf16[2,3,256,512]{3,2,1,0:T(8,128)(2,1)} %get-tuple-element.45.both_ref, bf16[3,256,128]{2,1,0:T(8,128)(2,1)} %get-tuple-element.40.refs_0_), custom_call_target="tpu_custom_call" | custom-call | flops 1610612736 | bytes 3145728 | tf_op jit(solution)/shard_map/forward/pallas_call | solution.py:320
  100.8 7.2 %all-to-all-start.2 = ((bf16[16,64,256]{2,1,0:T(8,128)(2,1)}), bf16[16,64,256]{2,1,0:T(8,128)(2,1)S(1)}, u32[]{:S(2)}, u32[]{:S(2)}) async-start(bf16[16,64,256]{2,1,0:T(8,128)(2,1)} %bitcast.15), calls=%async_computation.2 | async-start | bytes 1048576 | tf_op jit(solution)/shard_map/all_to_all | solution.py:583
  112.5 5.2 %collective-permute-done.15.refs_4_ = bf16[3,256,128]{2,1,0:T(8,128)(2,1)S(1)} collective-permute-done((bf16[3,256,128]{2,1,0:T(8,128)(2,1)S(1)}, bf16[3,256,128]{2,1,0:T(8,128)(2,1)S(1)}, u32[]{:S(2)}, u32[]{:S(2)}) %collective-permute-start.15) | collective-permute-done | bytes 196640 | tf_op jit(solution)/shard_map/ppermute | solution.py:549
  121.6 14.0 %close.1 = (bf16[2,3,256,512]{3,2,1,0:T(8,128)(2,1)}, bf16[2,3,256,128]{3,2,1,0:T(8,128)(2,1)S(1)}, bf16[1024,256]{1,0:T(8,128)(2,1)}, f32[2,16,64,256]{3,2,1,0:T(8,128)}) custom-call(s32[5]{0:T(128)S(1)} %copy-done.1, bf16[3,256,128]{2,1,0:T(8,128)(2,1)S(1)} %add_convert_fusion.refs_1_, bf16[3,256,128]{2,1,0:T(8,128)(2,1)S(1)} %collective-permute-done.13.refs_2_, ...), custom_call_target="tpu_custom_call" | custom-call | flops 6140612608 | bytes 10485760 | tf_op jit(solution)/shard_map/close/pallas_call | solution.py:365
  140.9 8.3 %all-to-all-start.3 = ((bf16[16,64,256]{2,1,0:T(8,128)(2,1)}), bf16[16,64,256]{2,1,0:T(8,128)(2,1)S(1)}, u32[]{:S(2)}, u32[]{:S(2)}) async-start(bf16[16,64,256]{2,1,0:T(8,128)(2,1)} %bitcast.16), calls=%async_computation.3 | async-start | bytes 1048576 | tf_op jit(solution)/shard_map/all_to_all | solution.py:589
  149.3 8.7 %collective-permute-done.22.refs_3_ = bf16[2,3,256,128]{3,2,1,0:T(8,128)(2,1)S(1)} collective-permute-done((bf16[2,3,256,128]{3,2,1,0:T(8,128)(2,1)S(1)}, bf16[2,3,256,128]{3,2,1,0:T(8,128)(2,1)S(1)}, u32[]{:S(2)}, u32[]{:S(2)}) %collective-permute-start.22) | collective-permute-done | bytes 393248 | tf_op jit(solution)/shard_map/ppermute | solution.py:587
  158.0 2.8 %collective-permute-start.25 = (bf16[2,3,256,128]{3,2,1,0:T(8,128)(2,1)S(1)}, bf16[2,3,256,128]{3,2,1,0:T(8,128)(2,1)S(1)}, u32[]{:S(2)}, u32[]{:S(2)}) collective-permute-start(bf16[2,3,256,128]{3,2,1,0:T(8,128)(2,1)S(1)} %collective-permute-done.22.refs_3_), channel_id=1, source_target_pairs={{1,33},{9,41},{16,48},{24,56},{33,65},{41,73},{48,80},{56,88},{65,... | collective-permute-start | bytes 1179656 | tf_op jit(solution)/shard_map/ppermute | solution.py:591
  160.8 5.1 %collective-permute-start.24 = (bf16[2,3,256,128]{3,2,1,0:T(8,128)(2,1)S(1)}, bf16[2,3,256,128]{3,2,1,0:T(8,128)(2,1)S(1)}, u32[]{:S(2)}, u32[]{:S(2)}) collective-permute-start(bf16[2,3,256,128]{3,2,1,0:T(8,128)(2,1)S(1)} %collective-permute-done.22.refs_3_), channel_id=1, source_target_pairs={{1,65},{9,73},{16,80},{24,88},{33,97},{41,105},{48,112},{56,120},{... | collective-permute-start | bytes 1179656 | tf_op jit(solution)/shard_map/ppermute | solution.py:591
  167.9 3.7 %all-to-all-done.3.refs_7_ = bf16[16,64,256]{2,1,0:T(8,128)(2,1)S(1)} async-done(((bf16[16,64,256]{2,1,0:T(8,128)(2,1)}), bf16[16,64,256]{2,1,0:T(8,128)(2,1)S(1)}, u32[]{:S(2)}, u32[]{:S(2)}) %all-to-all-start.3) | async-done | bytes 524320 | tf_op jit(solution)/shard_map/all_to_all | solution.py:589
  171.6 2.3 %collective-permute-done.24.refs_5_ = bf16[2,3,256,128]{3,2,1,0:T(8,128)(2,1)S(1)} collective-permute-done((bf16[2,3,256,128]{3,2,1,0:T(8,128)(2,1)S(1)}, bf16[2,3,256,128]{3,2,1,0:T(8,128)(2,1)S(1)}, u32[]{:S(2)}, u32[]{:S(2)}) %collective-permute-start.24) | collective-permute-done | bytes 393248 | tf_op jit(solution)/shard_map/ppermute | solution.py:591
  175.9 4.5 %finish.1 = (f32[2,256,1024]{2,1,0:T(8,128)}, f32[2,256,1024]{2,1,0:T(8,128)}, f32[2,256,1024]{2,1,0:T(8,128)}, f32[2,16,64,256]{3,2,1,0:T(8,128)}) custom-call(s32[5]{0:T(128)S(1)} %copy-done.1, bf16[2,3,256,512]{3,2,1,0:T(8,128)(2,1)} %get-tuple-element.46.refs_0_, ...), custom_call_target="tpu_custom_call", output_to_operand_aliasing={{3}: (9, {})} | custom-call | flops 1000000 | bytes 15728640 | tf_op jit(solution)/shard_map/finish/pallas_call | solution.py:501
  (72 shorter events, 33.2 us)
Async XLA Ops:
  0.6 13.5 %collective-permute-start = (f32[2,256,1024]{2,1,0:T(8,128)}, f32[2,256,1024]{2,1,0:T(8,128)S(1)}, u32[]{:S(2)}, u32[]{:S(2)}) collective-permute-start(f32[2,256,1024]{2,1,0:T(8,128)} %refs_0_.1), channel_id=1, source_target_pairs={{0,1},{1,0},{2,3},{3,2},{4,5},{5,4},{6,7},{7,6},{8,9},{9,8},{10,11... | collective-permute-start | bytes 6291464 | tf_op jit(solution)/shard_map/ppermute | solution.py:532
  0.7 13.4 %collective-permute-start.1 = (f32[2,256,1024]{2,1,0:T(8,128)}, f32[2,256,1024]{2,1,0:T(8,128)}, u32[]{:S(2)}, u32[]{:S(2)}) collective-permute-start(f32[2,256,1024]{2,1,0:T(8,128)} %refs_1_.1), channel_id=1, source_target_pairs={{0,1},{1,0},{2,3},{3,2},{4,5},{5,4},{6,7},{7,6},{8,9},{9,8},{10,11... | collective-permute-start | bytes 6291464 | tf_op jit(solution)/shard_map/ppermute | solution.py:532
  1.2 12.9 %collective-permute-start.2 = (f32[2,256,1024]{2,1,0:T(8,128)}, f32[2,256,1024]{2,1,0:T(8,128)}, u32[]{:S(2)}, u32[]{:S(2)}) collective-permute-start(f32[2,256,1024]{2,1,0:T(8,128)} %refs_2_.1), channel_id=1, source_target_pairs={{0,1},{1,0},{2,3},{3,2},{4,5},{5,4},{6,7},{7,6},{8,9},{9,8},{10,11... | collective-permute-start | bytes 6291464 | tf_op jit(solution)/shard_map/ppermute | solution.py:532
  4.0 17.1 %collective-permute-start.4 = (bf16[16,64,512]{2,1,0:T(8,128)(2,1)}, bf16[16,64,512]{2,1,0:T(8,128)(2,1)}, u32[]{:S(2)}, u32[]{:S(2)}) collective-permute-start(bf16[16,64,512]{2,1,0:T(8,128)(2,1)} %get-tuple-element.31.own_ref), channel_id=1, source_target_pairs={{0,1},{1,0},{2,3},{3,2},{4,5},{5,4},{6,7},{7,6},{8,9},{9,8},{10,11... | collective-permute-start | bytes 3145736 | tf_op jit(solution)/shard_map/ppermute | solution.py:532
  4.4 21.5 %all-to-all-start = ((bf16[16,64,512]{2,1,0:T(8,128)(2,1)}), bf16[16,64,512]{2,1,0:T(8,128)(2,1)S(1)}, u32[]{:S(2)}, u32[]{:S(2)}) async-start(bf16[16,64,512]{2,1,0:T(8,128)(2,1)} %get-tuple-element.29), calls=%async_computation | async-start | bytes 2097152 | tf_op jit(solution)/shard_map/all_to_all | solution.py:569
  25.9 48.0 %all-to-all-start.1 = ((bf16[16,64,1536]{2,1,0:T(8,128)(2,1)}), bf16[16,64,1536]{2,1,0:T(8,128)(2,1)}, u32[]{:S(2)}, u32[]{:S(2)}) async-start(bf16[16,64,1536]{2,1,0:T(8,128)(2,1)} %join.1), calls=%async_computation.1 | async-start | bytes 6291456 | tf_op jit(solution)/shard_map/all_to_all | solution.py:578
  44.0 9.6 %collective-permute-start.6 = (bf16[3,256,128]{2,1,0:T(8,128)(2,1)S(1)}, bf16[3,256,128]{2,1,0:T(8,128)(2,1)S(1)}, u32[]{:S(2)}, u32[]{:S(2)}) collective-permute-start(bf16[3,256,128]{2,1,0:T(8,128)(2,1)S(1)} %get-tuple-element.35), channel_id=1, source_target_pairs={{0,64},{32,96},{64,0},{96,32},{1,65},{33,97},{65,1},{97,33},{2,66}... | collective-permute-start | bytes 589832 | tf_op jit(solution)/shard_map/ppermute | solution.py:536
  48.0 9.4 %collective-permute-start.7 = (bf16[3,256,128]{2,1,0:T(8,128)(2,1)S(1)}, bf16[3,256,128]{2,1,0:T(8,128)(2,1)S(1)}, u32[]{:S(2)}, u32[]{:S(2)}) collective-permute-start(bf16[3,256,128]{2,1,0:T(8,128)(2,1)S(1)} %get-tuple-element.36), channel_id=1, source_target_pairs={{0,32},{32,64},{64,96},{96,0},{1,33},{33,65},{65,97},{97,1},{2,34}... | collective-permute-start | bytes 589832 | tf_op jit(solution)/shard_map/ppermute | solution.py:536
  49.0 9.1 %collective-permute-start.8 = (bf16[3,256,128]{2,1,0:T(8,128)(2,1)S(1)}, bf16[3,256,128]{2,1,0:T(8,128)(2,1)S(1)}, u32[]{:S(2)}, u32[]{:S(2)}) collective-permute-start(bf16[3,256,128]{2,1,0:T(8,128)(2,1)S(1)} %get-tuple-element.37), channel_id=1, source_target_pairs={{0,96},{32,0},{64,32},{96,64},{1,97},{33,1},{65,33},{97,65},{2,98}... | collective-permute-start | bytes 589832 | tf_op jit(solution)/shard_map/ppermute | solution.py:536
  91.4 16.7 %collective-permute-start.10 = (bf16[3,256,128]{2,1,0:T(8,128)(2,1)}, bf16[3,256,128]{2,1,0:T(8,128)(2,1)S(1)}, u32[]{:S(2)}, u32[]{:S(2)}) collective-permute-start(bf16[3,256,128]{2,1,0:T(8,128)(2,1)} %get-tuple-element.41), channel_id=1, source_target_pairs={{0,64},{32,96},{64,0},{96,32},{1,65},{33,97},{65,1},{97,33},{2,66}... | collective-permute-start | bytes 589832 | tf_op jit(solution)/shard_map/ppermute | solution.py:536
  92.9 15.2 %collective-permute-start.11 = (bf16[3,256,128]{2,1,0:T(8,128)(2,1)}, bf16[3,256,128]{2,1,0:T(8,128)(2,1)S(1)}, u32[]{:S(2)}, u32[]{:S(2)}) collective-permute-start(bf16[3,256,128]{2,1,0:T(8,128)(2,1)} %get-tuple-element.42), channel_id=1, source_target_pairs={{0,32},{32,64},{64,96},{96,0},{1,33},{33,65},{65,97},{97,1},{2,34}... | collective-permute-start | bytes 589832 | tf_op jit(solution)/shard_map/ppermute | solution.py:536
  95.8 12.3 %collective-permute-start.12 = (bf16[3,256,128]{2,1,0:T(8,128)(2,1)}, bf16[3,256,128]{2,1,0:T(8,128)(2,1)S(1)}, u32[]{:S(2)}, u32[]{:S(2)}) collective-permute-start(bf16[3,256,128]{2,1,0:T(8,128)(2,1)} %get-tuple-element.43), channel_id=1, source_target_pairs={{0,96},{32,0},{64,32},{96,64},{1,97},{33,1},{65,33},{97,65},{2,98}... | collective-permute-start | bytes 589832 | tf_op jit(solution)/shard_map/ppermute | solution.py:536
  100.8 19.3 %all-to-all-start.2 = ((bf16[16,64,256]{2,1,0:T(8,128)(2,1)}), bf16[16,64,256]{2,1,0:T(8,128)(2,1)S(1)}, u32[]{:S(2)}, u32[]{:S(2)}) async-start(bf16[16,64,256]{2,1,0:T(8,128)(2,1)} %bitcast.15), calls=%async_computation.2 | async-start | bytes 1048576 | tf_op jit(solution)/shard_map/all_to_all | solution.py:583
  108.2 9.5 %collective-permute-start.15 = (bf16[3,256,128]{2,1,0:T(8,128)(2,1)S(1)}, bf16[3,256,128]{2,1,0:T(8,128)(2,1)S(1)}, u32[]{:S(2)}, u32[]{:S(2)}) collective-permute-start(bf16[3,256,128]{2,1,0:T(8,128)(2,1)S(1)} %add_convert_fusion.refs_1_), channel_id=1, source_target_pairs={{0,32},{32,64},{64,96},{96,0},{1,33},{33,65},{65,97},{97,1},{2,34}... | collective-permute-start | bytes 589832 | tf_op jit(solution)/shard_map/ppermute | solution.py:549
  109.7 9.8 %collective-permute-start.14 = (bf16[3,256,128]{2,1,0:T(8,128)(2,1)S(1)}, bf16[3,256,128]{2,1,0:T(8,128)(2,1)S(1)}, u32[]{:S(2)}, u32[]{:S(2)}) collective-permute-start(bf16[3,256,128]{2,1,0:T(8,128)(2,1)S(1)} %add_convert_fusion.refs_1_), channel_id=1, source_target_pairs={{0,64},{32,96},{64,0},{96,32},{1,65},{33,97},{65,1},{97,33},{2,66}... | collective-permute-start | bytes 589832 | tf_op jit(solution)/shard_map/ppermute | solution.py:549
  111.8 8.4 %collective-permute-start.13 = (bf16[3,256,128]{2,1,0:T(8,128)(2,1)S(1)}, bf16[3,256,128]{2,1,0:T(8,128)(2,1)S(1)}, u32[]{:S(2)}, u32[]{:S(2)}) collective-permute-start(bf16[3,256,128]{2,1,0:T(8,128)(2,1)S(1)} %add_convert_fusion.refs_1_), channel_id=1, source_target_pairs={{0,96},{32,0},{64,32},{96,64},{1,97},{33,1},{65,33},{97,65},{2,98}... | collective-permute-start | bytes 589832 | tf_op jit(solution)/shard_map/ppermute | solution.py:549
  112.5 7.7 %collective-permute-start.16 = (bf16[3,256,128]{2,1,0:T(8,128)(2,1)S(1)}, bf16[3,256,128]{2,1,0:T(8,128)(2,1)S(1)}, u32[]{:S(2)}, u32[]{:S(2)}) collective-permute-start(bf16[3,256,128]{2,1,0:T(8,128)(2,1)S(1)} %add_convert_fusion.refs_1_), channel_id=1, source_target_pairs={{0,1},{1,0},{2,3},{3,2},{4,5},{5,4},{6,7},{7,6},{8,9},{9,8},{10,11... | collective-permute-start | bytes 589832 | tf_op jit(solution)/shard_map/ppermute | solution.py:532
  135.6 40.2 %collective-permute-start.21 = (bf16[2,3,256,512]{3,2,1,0:T(8,128)(2,1)}, bf16[2,3,256,512]{3,2,1,0:T(8,128)(2,1)}, u32[]{:S(2)}, u32[]{:S(2)}) collective-permute-start(bf16[2,3,256,512]{3,2,1,0:T(8,128)(2,1)} %get-tuple-element.46.refs_0_), channel_id=1, source_target_pairs={{0,24},{8,0},{17,9},{25,17},{2,26},{10,2},{19,11},{27,19},{4,28},{... | collective-permute-start | bytes 4718600 | tf_op jit(solution)/shard_map/ppermute | solution.py:588
  137.4 38.4 %collective-permute-start.20 = (bf16[2,3,256,512]{3,2,1,0:T(8,128)(2,1)}, bf16[2,3,256,512]{3,2,1,0:T(8,128)(2,1)}, u32[]{:S(2)}, u32[]{:S(2)}) collective-permute-start(bf16[2,3,256,512]{3,2,1,0:T(8,128)(2,1)} %get-tuple-element.46.refs_0_), channel_id=1, source_target_pairs={{0,8},{8,16},{17,25},{25,1},{2,10},{10,18},{19,27},{27,3},{4,12},{... | collective-permute-start | bytes 4718600 | tf_op jit(solution)/shard_map/ppermute | solution.py:588
  138.7 19.2 %collective-permute-start.22 = (bf16[2,3,256,128]{3,2,1,0:T(8,128)(2,1)S(1)}, bf16[2,3,256,128]{3,2,1,0:T(8,128)(2,1)S(1)}, u32[]{:S(2)}, u32[]{:S(2)}) collective-permute-start(bf16[2,3,256,128]{3,2,1,0:T(8,128)(2,1)S(1)} %get-tuple-element.47), channel_id=1, source_target_pairs={{1,16},{9,24},{16,1},{24,9},{3,18},{11,26},{18,3},{26,11},{5,20},{... | collective-permute-start | bytes 1179656 | tf_op jit(solution)/shard_map/ppermute | solution.py:587
  140.9 30.7 %all-to-all-start.3 = ((bf16[16,64,256]{2,1,0:T(8,128)(2,1)}), bf16[16,64,256]{2,1,0:T(8,128)(2,1)S(1)}, u32[]{:S(2)}, u32[]{:S(2)}) async-start(bf16[16,64,256]{2,1,0:T(8,128)(2,1)} %bitcast.16), calls=%async_computation.3 | async-start | bytes 1048576 | tf_op jit(solution)/shard_map/all_to_all | solution.py:589
  158.0 13.6 %collective-permute-start.25 = (bf16[2,3,256,128]{3,2,1,0:T(8,128)(2,1)S(1)}, bf16[2,3,256,128]{3,2,1,0:T(8,128)(2,1)S(1)}, u32[]{:S(2)}, u32[]{:S(2)}) collective-permute-start(bf16[2,3,256,128]{3,2,1,0:T(8,128)(2,1)S(1)} %collective-permute-done.22.refs_3_), channel_id=1, source_target_pairs={{1,33},{9,41},{16,48},{24,56},{33,65},{41,73},{48,80},{56,88},{65,... | collective-permute-start | bytes 1179656 | tf_op jit(solution)/shard_map/ppermute | solution.py:591
  160.8 13.1 %collective-permute-start.24 = (bf16[2,3,256,128]{3,2,1,0:T(8,128)(2,1)S(1)}, bf16[2,3,256,128]{3,2,1,0:T(8,128)(2,1)S(1)}, u32[]{:S(2)}, u32[]{:S(2)}) collective-permute-start(bf16[2,3,256,128]{3,2,1,0:T(8,128)(2,1)S(1)} %collective-permute-done.22.refs_3_), channel_id=1, source_target_pairs={{1,65},{9,73},{16,80},{24,88},{33,97},{41,105},{48,112},{56,120},{... | collective-permute-start | bytes 1179656 | tf_op jit(solution)/shard_map/ppermute | solution.py:591
  165.9 9.9 %collective-permute-start.23 = (bf16[2,3,256,128]{3,2,1,0:T(8,128)(2,1)S(1)}, bf16[2,3,256,128]{3,2,1,0:T(8,128)(2,1)S(1)}, u32[]{:S(2)}, u32[]{:S(2)}) collective-permute-start(bf16[2,3,256,128]{3,2,1,0:T(8,128)(2,1)S(1)} %collective-permute-done.22.refs_3_), channel_id=1, source_target_pairs={{1,97},{9,105},{16,112},{24,120},{33,1},{41,9},{48,16},{56,24},{65... | collective-permute-start | bytes 1179656 | tf_op jit(solution)/shard_map/ppermute | solution.py:591
  (17 other events, 103.3 us)

commit v4 on v3

--- a/solution.py
+++ b/solution.py
@@ -276,7 +276,7 @@
         in_specs=[SSPEC] + [ANYSPEC] * 2 + [HBMSPEC, VSPEC, HBMSPEC],
         out_specs=[HBMSPEC] * 2 + [VSPEC] * 4,
         scratch_shapes=NS_SCRATCH + GRAD_SCRATCH + [pltpu.SemaphoreType.DMA((2,))] + GRAD_PIECES,
-        compiler_params=params(56),
+        compiler_params=params(50),
         name="turn",
         cost_estimate=cost(NS_FLOPS + 12 * 2 * TOK * DH * HALF, 14 * MIB, 2 * TOK * HALF),
     )(place, *chunks, weight, step, rest)

time: 181 us -> 180 us (level)
    pallas_call x1, Pallas kernels: 16.6 us -> 14.7 us  [turn(): pl.pallas_call(turn_kernel, out_shape=[BOTH, jax.ShapeDtypeStruct((3, 8,...]
where the time goes in v4:
time: 180 us
  starting transfers between devices  63.9 us (36%)
  Pallas kernels  56.5 us (31%)
  waiting for transfers between devices  39.7 us (22%)
  blocking collectives  13.3 us (7%)
  local copies, waits for them, and re-layouts  4.96 us (3%)
    pallas_call x1, Pallas kernels, turn(): pl.pallas_call(turn_kernel, out_shape=[BOTH, jax.ShapeDtypeStruct((3, 8,...  14.7 us
    pallas_call x1, Pallas kernels, close(): pl.pallas_call(close_kernel, out_shape=[BOTH, jax.ShapeDtypeStruct((2, 3,...  14 us
    all_gather x1, blocking collectives, gather(): whole = lax.all_gather(value, 'z')  13.3 us
    ppermute x6, starting transfers between devices, sum_up(): received = [lax.ppermute(partial[far], 'z', ring(far)) for far in (2, 1, 3)]  12.3 us
    ppermute x3, starting transfers between devices, shards(): lax.ppermute(quarters[0], ('z', 'y', 'c'), z_pairs(4 - far))  9.9 us
    ppermute x1, waiting for transfers between devices, shards(): quarters = [move(quarter, perm=y_pairs(2, across=1))]  8.68 us
    all_to_all x1, starting transfers between devices, shards(): late = exchange(result.reshape(16, 64, DH))  8.33 us
    all_to_all x1, starting transfers between devices, shards(): rest = exchange(after(second, first)).reshape(TOK, 6 * DH)  8.31 us
  transfers between devices with their start and end apart: 30, of which 16 were waited for; matrix products, arithmetic and copies ran while one was open for 1% of the time, Pallas kernels for 13%

profile of v4, /device:TPU:20, one launch (start us, length us, event | category | flops | bytes accessed | tf_op | source)
XLA Modules:
  0.0 179.6 jit_solution(12712293992994234805)
XLA Ops:
  1.3 2.7 %pack.1 = (bf16[16,64,512]{2,1,0:T(8,128)(2,1)}, bf16[16,64,512]{2,1,0:T(8,128)(2,1)}) custom-call(bf16[2,16,64,256]{3,2,1,0:T(8,128)(2,1)} %key_ref.1, bf16[2,16,64,256]{3,2,1,0:T(8,128)(2,1)} %value_ref.1, bf16[2,16,64]{2,1,0:T(8,128)(2,1)} %rate_ref.1), custom_call_target="tpu_custom_call" | custom-call | flops 1 | bytes 1 | tf_op jit(solution)/shard_map/pack/pallas_call | solution.py:60
  4.4 7.2 %all-to-all-start = ((bf16[16,64,512]{2,1,0:T(8,128)(2,1)}), bf16[16,64,512]{2,1,0:T(8,128)(2,1)S(1)}, u32[]{:S(2)}, u32[]{:S(2)}) async-start(bf16[16,64,512]{2,1,0:T(8,128)(2,1)} %get-tuple-element.29), calls=%async_computation | async-start | bytes 2097152 | tf_op jit(solution)/shard_map/all_to_all | solution.py:569
  15.5 5.7 %prepare.1 = (f32[3,8,256,128]{3,2,1,0:T(8,128)}, bf16[2,3,256,512]{3,2,1,0:T(8,128)(2,1)}, f32[8,128]{1,0:T(8,128)}) custom-call(s32[5]{0:T(128)} %stack.27.place_ref.refs_0_, f32[2,256,1024]{2,1,0:T(8,128)} %refs_0_.1, f32[2,256,1024]{2,1,0:T(8,128)} %refs_1_.1, f32[2,256,1024]{2,1,0:T(8,128)} %refs_2_.1, f32[2,256,1024]{2,1,0:T(8,128)} %copy-done.5, ...), custom_call_target="tpu_custom_call" | custom-call | flops 1 | bytes 1 | tf_op jit(solution)/shard_map/prepare/pallas_call | solution.py:433
  21.2 3.2 %join.1 = bf16[16,64,1536]{2,1,0:T(8,128)(2,1)} custom-call(bf16[16,64,512]{2,1,0:T(8,128)(2,1)} %get-tuple-element.31.own_ref, bf16[16,64,512]{2,1,0:T(8,128)(2,1)} %collective-permute-done.4.peer_ref, bf16[2,16,64,256]{3,2,1,0:T(8,128)(2,1)} %queries_ref.1, f32[8,128]{1,0:T(8,128)} %get-tuple-element.30.refs_0_.refs_4_.refs_10_), custom_call_target="tpu_custom_call" | custom-call | flops 1 | bytes 1 | tf_op jit(solution)/shard_map/join/pallas_call | solution.py:83
  25.9 8.3 %all-to-all-start.1 = ((bf16[16,64,1536]{2,1,0:T(8,128)(2,1)}), bf16[16,64,1536]{2,1,0:T(8,128)(2,1)}, u32[]{:S(2)}, u32[]{:S(2)}) async-start(bf16[16,64,1536]{2,1,0:T(8,128)(2,1)} %join.1), calls=%async_computation.1 | async-start | bytes 6291456 | tf_op jit(solution)/shard_map/all_to_all | solution.py:578
  34.2 2.7 %collective-permute-done.5.peer_ref = bf16[1024,512]{1,0:T(8,128)(2,1)S(1)} collective-permute-done((bf16[1024,512]{1,0:T(8,128)(2,1)S(1)}, bf16[1024,512]{1,0:T(8,128)(2,1)S(1)}, u32[]{:S(2)}, u32[]{:S(2)}) %collective-permute-start.5) | collective-permute-done | bytes 1048608 | tf_op jit(solution)/shard_map/ppermute | solution.py:532
  36.9 7.3 %grads.1 = (bf16[3,256,128]{2,1,0:T(8,128)(2,1)S(1)}, bf16[3,256,128]{2,1,0:T(8,128)(2,1)S(1)}, bf16[3,256,128]{2,1,0:T(8,128)(2,1)S(1)}, bf16[3,256,128]{2,1,0:T(8,128)(2,1)S(1)}) custom-call(s32[5]{0:T(128)S(1)} %copy-done.2, bf16[1024,512]{1,0:T(8,128)(2,1)S(1)} %bitcast.12, bf16[1024,512]{1,0:T(8,128)(2,1)S(1)} %collective-permute-done.5.peer_ref, ...), custom_call_target="tpu_custom_call" | custom-call | flops 3221225472 | bytes 4194304 | tf_op jit(solution)/shard_map/grads/pallas_call | solution.py:152
  44.2 4.0 %collective-permute-start.6 = (bf16[3,256,128]{2,1,0:T(8,128)(2,1)S(1)}, bf16[3,256,128]{2,1,0:T(8,128)(2,1)S(1)}, u32[]{:S(2)}, u32[]{:S(2)}) collective-permute-start(bf16[3,256,128]{2,1,0:T(8,128)(2,1)S(1)} %get-tuple-element.35), channel_id=1, source_target_pairs={{0,64},{32,96},{64,0},{96,32},{1,65},{33,97},{65,1},{97,33},{2,66}... | collective-permute-start | bytes 589832 | tf_op jit(solution)/shard_map/ppermute | solution.py:536
  51.4 2.5 %collective-permute-done.6 = bf16[3,256,128]{2,1,0:T(8,128)(2,1)S(1)} collective-permute-done((bf16[3,256,128]{2,1,0:T(8,128)(2,1)S(1)}, bf16[3,256,128]{2,1,0:T(8,128)(2,1)S(1)}, u32[]{:S(2)}, u32[]{:S(2)}) %collective-permute-start.6) | collective-permute-done | bytes 196640 | tf_op jit(solution)/shard_map/ppermute | solution.py:536
  53.8 3.7 %collective-permute-done.7 = bf16[3,256,128]{2,1,0:T(8,128)(2,1)S(1)} collective-permute-done((bf16[3,256,128]{2,1,0:T(8,128)(2,1)S(1)}, bf16[3,256,128]{2,1,0:T(8,128)(2,1)S(1)}, u32[]{:S(2)}, u32[]{:S(2)}) %collective-permute-start.7) | collective-permute-done | bytes 196640 | tf_op jit(solution)/shard_map/ppermute | solution.py:536
  58.4 13.3 %all-gather = bf16[12,256,128]{2,1,0:T(8,128)(2,1)S(1)} all-gather(bf16[3,256,128]{2,1,0:T(8,128)(2,1)S(1)} %add_convert_fusion.1), channel_id=2, replica_groups=mesh['z'=4,'y'=4,'x'=4,'c'=2] {'z'}, dimensions={0}, use_global_device_ids=true | all-gather | bytes 983040 | tf_op jit(solution)/shard_map/all_gather | solution.py:544
  74.0 14.7 %turn.1 = (bf16[2,3,256,512]{3,2,1,0:T(8,128)(2,1)S(1)}, f32[3,8,256,128]{3,2,1,0:T(8,128)}, bf16[3,256,128]{2,1,0:T(8,128)(2,1)S(1)}, bf16[3,256,128]{2,1,0:T(8...) custom-call(s32[5]{0:T(128)S(1)} %copy-done.2, bf16[4,3,256,128]{3,2,1,0:T(8,128)(2,1)S(1)} %bitcast.14, ...), custom_call_target="tpu_custom_call" | custom-call | flops 7751225344 | bytes 14680064 | tf_op jit(solution)/shard_map/turn/pallas_call | solution.py:272
  92.5 2.4 %collective-permute-start.11 = (bf16[3,256,128]{2,1,0:T(8,128)(2,1)S(1)}, bf16[3,256,128]{2,1,0:T(8,128)(2,1)S(1)}, u32[]{:S(2)}, u32[]{:S(2)}) collective-permute-start(bf16[3,256,128]{2,1,0:T(8,128)(2,1)S(1)} %get-tuple-element.42), channel_id=1, source_target_pairs={{0,32},{32,64},{64,96},{96,0},{1,33},{33,65},{65,97},{97,1},{2,34}... | collective-permute-start | bytes 589832 | tf_op jit(solution)/shard_map/ppermute | solution.py:536
  95.7 4.4 %forward.1 = bf16[1024,256]{1,0:T(8,128)(2,1)} custom-call(bf16[1024,1536]{1,0:T(8,128)(2,1)} %bitcast.8.refs_5_.rest_ref.refs_11_, bf16[2,3,256,512]{3,2,1,0:T(8,128)(2,1)} %copy-done.4, bf16[3,256,128]{2,1,0:T(8,128)(2,1)} %copy-done), custom_call_target="tpu_custom_call" | custom-call | flops 1610612736 | bytes 3145728 | tf_op jit(solution)/shard_map/forward/pallas_call | solution.py:320
  100.1 7.2 %all-to-all-start.2 = ((bf16[16,64,256]{2,1,0:T(8,128)(2,1)}), bf16[16,64,256]{2,1,0:T(8,128)(2,1)S(1)}, u32[]{:S(2)}, u32[]{:S(2)}) async-start(bf16[16,64,256]{2,1,0:T(8,128)(2,1)} %bitcast.15), calls=%async_computation.2 | async-start | bytes 1048576 | tf_op jit(solution)/shard_map/all_to_all | solution.py:583
  111.6 5.2 %collective-permute-done.15.refs_4_ = bf16[3,256,128]{2,1,0:T(8,128)(2,1)S(1)} collective-permute-done((bf16[3,256,128]{2,1,0:T(8,128)(2,1)S(1)}, bf16[3,256,128]{2,1,0:T(8,128)(2,1)S(1)}, u32[]{:S(2)}, u32[]{:S(2)}) %collective-permute-start.15) | collective-permute-done | bytes 196640 | tf_op jit(solution)/shard_map/ppermute | solution.py:549
  120.7 14.0 %close.1 = (bf16[2,3,256,512]{3,2,1,0:T(8,128)(2,1)}, bf16[2,3,256,128]{3,2,1,0:T(8,128)(2,1)S(1)}, bf16[1024,256]{1,0:T(8,128)(2,1)}, f32[2,16,64,256]{3,2,1,0:T(8,128)}) custom-call(s32[5]{0:T(128)S(1)} %copy-done.2, bf16[3,256,128]{2,1,0:T(8,128)(2,1)S(1)} %add_convert_fusion.refs_1_, bf16[3,256,128]{2,1,0:T(8,128)(2,1)S(1)} %collective-permute-done.13.refs_2_, ...), custom_call_target="tpu_custom_call" | custom-call | flops 6140612608 | bytes 10485760 | tf_op jit(solution)/shard_map/close/pallas_call | solution.py:365
  140.0 8.3 %all-to-all-start.3 = ((bf16[16,64,256]{2,1,0:T(8,128)(2,1)}), bf16[16,64,256]{2,1,0:T(8,128)(2,1)S(1)}, u32[]{:S(2)}, u32[]{:S(2)}) async-start(bf16[16,64,256]{2,1,0:T(8,128)(2,1)} %bitcast.16), calls=%async_computation.3 | async-start | bytes 1048576 | tf_op jit(solution)/shard_map/all_to_all | solution.py:589
  148.4 8.7 %collective-permute-done.22.refs_3_ = bf16[2,3,256,128]{3,2,1,0:T(8,128)(2,1)S(1)} collective-permute-done((bf16[2,3,256,128]{3,2,1,0:T(8,128)(2,1)S(1)}, bf16[2,3,256,128]{3,2,1,0:T(8,128)(2,1)S(1)}, u32[]{:S(2)}, u32[]{:S(2)}) %collective-permute-start.22) | collective-permute-done | bytes 393248 | tf_op jit(solution)/shard_map/ppermute | solution.py:587
  157.0 2.9 %collective-permute-start.25 = (bf16[2,3,256,128]{3,2,1,0:T(8,128)(2,1)S(1)}, bf16[2,3,256,128]{3,2,1,0:T(8,128)(2,1)S(1)}, u32[]{:S(2)}, u32[]{:S(2)}) collective-permute-start(bf16[2,3,256,128]{3,2,1,0:T(8,128)(2,1)S(1)} %collective-permute-done.22.refs_3_), channel_id=1, source_target_pairs={{1,33},{9,41},{16,48},{24,56},{33,65},{41,73},{48,80},{56,88},{65,... | collective-permute-start | bytes 1179656 | tf_op jit(solution)/shard_map/ppermute | solution.py:591
  159.9 5.1 %collective-permute-start.24 = (bf16[2,3,256,128]{3,2,1,0:T(8,128)(2,1)S(1)}, bf16[2,3,256,128]{3,2,1,0:T(8,128)(2,1)S(1)}, u32[]{:S(2)}, u32[]{:S(2)}) collective-permute-start(bf16[2,3,256,128]{3,2,1,0:T(8,128)(2,1)S(1)} %collective-permute-done.22.refs_3_), channel_id=1, source_target_pairs={{1,65},{9,73},{16,80},{24,88},{33,97},{41,105},{48,112},{56,120},{... | collective-permute-start | bytes 1179656 | tf_op jit(solution)/shard_map/ppermute | solution.py:591
  167.0 3.7 %all-to-all-done.3.refs_7_ = bf16[16,64,256]{2,1,0:T(8,128)(2,1)S(1)} async-done(((bf16[16,64,256]{2,1,0:T(8,128)(2,1)}), bf16[16,64,256]{2,1,0:T(8,128)(2,1)S(1)}, u32[]{:S(2)}, u32[]{:S(2)}) %all-to-all-start.3) | async-done | bytes 524320 | tf_op jit(solution)/shard_map/all_to_all | solution.py:589
  170.7 2.3 %collective-permute-done.24.refs_5_ = bf16[2,3,256,128]{3,2,1,0:T(8,128)(2,1)S(1)} collective-permute-done((bf16[2,3,256,128]{3,2,1,0:T(8,128)(2,1)S(1)}, bf16[2,3,256,128]{3,2,1,0:T(8,128)(2,1)S(1)}, u32[]{:S(2)}, u32[]{:S(2)}) %collective-permute-start.24) | collective-permute-done | bytes 393248 | tf_op jit(solution)/shard_map/ppermute | solution.py:591
  174.9 4.5 %finish.1 = (f32[2,256,1024]{2,1,0:T(8,128)}, f32[2,256,1024]{2,1,0:T(8,128)}, f32[2,256,1024]{2,1,0:T(8,128)}, f32[2,16,64,256]{3,2,1,0:T(8,128)}) custom-call(s32[5]{0:T(128)S(1)} %copy-done.2, bf16[2,3,256,512]{3,2,1,0:T(8,128)(2,1)} %get-tuple-element.46.refs_0_, ...), custom_call_target="tpu_custom_call", output_to_operand_aliasing={{3}: (9, {})} | custom-call | flops 1000000 | bytes 15728640 | tf_op jit(solution)/shard_map/finish/pallas_call | solution.py:501
  (70 shorter events, 34.6 us)
Async XLA Ops:
  0.6 13.5 %collective-permute-start = (f32[2,256,1024]{2,1,0:T(8,128)}, f32[2,256,1024]{2,1,0:T(8,128)S(1)}, u32[]{:S(2)}, u32[]{:S(2)}) collective-permute-start(f32[2,256,1024]{2,1,0:T(8,128)} %refs_0_.1), channel_id=1, source_target_pairs={{0,1},{1,0},{2,3},{3,2},{4,5},{5,4},{6,7},{7,6},{8,9},{9,8},{10,11... | collective-permute-start | bytes 6291464 | tf_op jit(solution)/shard_map/ppermute | solution.py:532
  0.7 13.4 %collective-permute-start.1 = (f32[2,256,1024]{2,1,0:T(8,128)}, f32[2,256,1024]{2,1,0:T(8,128)}, u32[]{:S(2)}, u32[]{:S(2)}) collective-permute-start(f32[2,256,1024]{2,1,0:T(8,128)} %refs_1_.1), channel_id=1, source_target_pairs={{0,1},{1,0},{2,3},{3,2},{4,5},{5,4},{6,7},{7,6},{8,9},{9,8},{10,11... | collective-permute-start | bytes 6291464 | tf_op jit(solution)/shard_map/ppermute | solution.py:532
  1.2 12.9 %collective-permute-start.2 = (f32[2,256,1024]{2,1,0:T(8,128)}, f32[2,256,1024]{2,1,0:T(8,128)}, u32[]{:S(2)}, u32[]{:S(2)}) collective-permute-start(f32[2,256,1024]{2,1,0:T(8,128)} %refs_2_.1), channel_id=1, source_target_pairs={{0,1},{1,0},{2,3},{3,2},{4,5},{5,4},{6,7},{7,6},{8,9},{9,8},{10,11... | collective-permute-start | bytes 6291464 | tf_op jit(solution)/shard_map/ppermute | solution.py:532
  4.0 17.2 %collective-permute-start.4 = (bf16[16,64,512]{2,1,0:T(8,128)(2,1)}, bf16[16,64,512]{2,1,0:T(8,128)(2,1)}, u32[]{:S(2)}, u32[]{:S(2)}) collective-permute-start(bf16[16,64,512]{2,1,0:T(8,128)(2,1)} %get-tuple-element.31.own_ref), channel_id=1, source_target_pairs={{0,1},{1,0},{2,3},{3,2},{4,5},{5,4},{6,7},{7,6},{8,9},{9,8},{10,11... | collective-permute-start | bytes 3145736 | tf_op jit(solution)/shard_map/ppermute | solution.py:532
  4.4 21.5 %all-to-all-start = ((bf16[16,64,512]{2,1,0:T(8,128)(2,1)}), bf16[16,64,512]{2,1,0:T(8,128)(2,1)S(1)}, u32[]{:S(2)}, u32[]{:S(2)}) async-start(bf16[16,64,512]{2,1,0:T(8,128)(2,1)} %get-tuple-element.29), calls=%async_computation | async-start | bytes 2097152 | tf_op jit(solution)/shard_map/all_to_all | solution.py:569
  25.9 48.1 %all-to-all-start.1 = ((bf16[16,64,1536]{2,1,0:T(8,128)(2,1)}), bf16[16,64,1536]{2,1,0:T(8,128)(2,1)}, u32[]{:S(2)}, u32[]{:S(2)}) async-start(bf16[16,64,1536]{2,1,0:T(8,128)(2,1)} %join.1), calls=%async_computation.1 | async-start | bytes 6291456 | tf_op jit(solution)/shard_map/all_to_all | solution.py:578
  44.2 9.6 %collective-permute-start.6 = (bf16[3,256,128]{2,1,0:T(8,128)(2,1)S(1)}, bf16[3,256,128]{2,1,0:T(8,128)(2,1)S(1)}, u32[]{:S(2)}, u32[]{:S(2)}) collective-permute-start(bf16[3,256,128]{2,1,0:T(8,128)(2,1)S(1)} %get-tuple-element.35), channel_id=1, source_target_pairs={{0,64},{32,96},{64,0},{96,32},{1,65},{33,97},{65,1},{97,33},{2,66}... | collective-permute-start | bytes 589832 | tf_op jit(solution)/shard_map/ppermute | solution.py:536
  48.2 9.4 %collective-permute-start.7 = (bf16[3,256,128]{2,1,0:T(8,128)(2,1)S(1)}, bf16[3,256,128]{2,1,0:T(8,128)(2,1)S(1)}, u32[]{:S(2)}, u32[]{:S(2)}) collective-permute-start(bf16[3,256,128]{2,1,0:T(8,128)(2,1)S(1)} %get-tuple-element.36), channel_id=1, source_target_pairs={{0,32},{32,64},{64,96},{96,0},{1,33},{33,65},{65,97},{97,1},{2,34}... | collective-permute-start | bytes 589832 | tf_op jit(solution)/shard_map/ppermute | solution.py:536
  49.2 9.1 %collective-permute-start.8 = (bf16[3,256,128]{2,1,0:T(8,128)(2,1)S(1)}, bf16[3,256,128]{2,1,0:T(8,128)(2,1)S(1)}, u32[]{:S(2)}, u32[]{:S(2)}) collective-permute-start(bf16[3,256,128]{2,1,0:T(8,128)(2,1)S(1)} %get-tuple-element.37), channel_id=1, source_target_pairs={{0,96},{32,0},{64,32},{96,64},{1,97},{33,1},{65,33},{97,65},{2,98}... | collective-permute-start | bytes 589832 | tf_op jit(solution)/shard_map/ppermute | solution.py:536
  90.6 16.8 %collective-permute-start.10 = (bf16[3,256,128]{2,1,0:T(8,128)(2,1)S(1)}, bf16[3,256,128]{2,1,0:T(8,128)(2,1)S(1)}, u32[]{:S(2)}, u32[]{:S(2)}) collective-permute-start(bf16[3,256,128]{2,1,0:T(8,128)(2,1)S(1)} %get-tuple-element.41), channel_id=1, source_target_pairs={{0,64},{32,96},{64,0},{96,32},{1,65},{33,97},{65,1},{97,33},{2,66}... | collective-permute-start | bytes 589832 | tf_op jit(solution)/shard_map/ppermute | solution.py:536
  92.5 14.9 %collective-permute-start.11 = (bf16[3,256,128]{2,1,0:T(8,128)(2,1)S(1)}, bf16[3,256,128]{2,1,0:T(8,128)(2,1)S(1)}, u32[]{:S(2)}, u32[]{:S(2)}) collective-permute-start(bf16[3,256,128]{2,1,0:T(8,128)(2,1)S(1)} %get-tuple-element.42), channel_id=1, source_target_pairs={{0,32},{32,64},{64,96},{96,0},{1,33},{33,65},{65,97},{97,1},{2,34}... | collective-permute-start | bytes 589832 | tf_op jit(solution)/shard_map/ppermute | solution.py:536
  94.9 12.5 %collective-permute-start.12 = (bf16[3,256,128]{2,1,0:T(8,128)(2,1)S(1)}, bf16[3,256,128]{2,1,0:T(8,128)(2,1)S(1)}, u32[]{:S(2)}, u32[]{:S(2)}) collective-permute-start(bf16[3,256,128]{2,1,0:T(8,128)(2,1)S(1)} %get-tuple-element.43), channel_id=1, source_target_pairs={{0,96},{32,0},{64,32},{96,64},{1,97},{33,1},{65,33},{97,65},{2,98}... | collective-permute-start | bytes 589832 | tf_op jit(solution)/shard_map/ppermute | solution.py:536
  100.1 19.1 %all-to-all-start.2 = ((bf16[16,64,256]{2,1,0:T(8,128)(2,1)}), bf16[16,64,256]{2,1,0:T(8,128)(2,1)S(1)}, u32[]{:S(2)}, u32[]{:S(2)}) async-start(bf16[16,64,256]{2,1,0:T(8,128)(2,1)} %bitcast.15), calls=%async_computation.2 | async-start | bytes 1048576 | tf_op jit(solution)/shard_map/all_to_all | solution.py:583
  107.5 9.3 %collective-permute-start.15 = (bf16[3,256,128]{2,1,0:T(8,128)(2,1)S(1)}, bf16[3,256,128]{2,1,0:T(8,128)(2,1)S(1)}, u32[]{:S(2)}, u32[]{:S(2)}) collective-permute-start(bf16[3,256,128]{2,1,0:T(8,128)(2,1)S(1)} %add_convert_fusion.refs_1_), channel_id=1, source_target_pairs={{0,32},{32,64},{64,96},{96,0},{1,33},{33,65},{65,97},{97,1},{2,34}... | collective-permute-start | bytes 589832 | tf_op jit(solution)/shard_map/ppermute | solution.py:549
  108.8 9.8 %collective-permute-start.14 = (bf16[3,256,128]{2,1,0:T(8,128)(2,1)S(1)}, bf16[3,256,128]{2,1,0:T(8,128)(2,1)S(1)}, u32[]{:S(2)}, u32[]{:S(2)}) collective-permute-start(bf16[3,256,128]{2,1,0:T(8,128)(2,1)S(1)} %add_convert_fusion.refs_1_), channel_id=1, source_target_pairs={{0,64},{32,96},{64,0},{96,32},{1,65},{33,97},{65,1},{97,33},{2,66}... | collective-permute-start | bytes 589832 | tf_op jit(solution)/shard_map/ppermute | solution.py:549
  110.9 8.4 %collective-permute-start.13 = (bf16[3,256,128]{2,1,0:T(8,128)(2,1)S(1)}, bf16[3,256,128]{2,1,0:T(8,128)(2,1)S(1)}, u32[]{:S(2)}, u32[]{:S(2)}) collective-permute-start(bf16[3,256,128]{2,1,0:T(8,128)(2,1)S(1)} %add_convert_fusion.refs_1_), channel_id=1, source_target_pairs={{0,96},{32,0},{64,32},{96,64},{1,97},{33,1},{65,33},{97,65},{2,98}... | collective-permute-start | bytes 589832 | tf_op jit(solution)/shard_map/ppermute | solution.py:549
  111.6 7.7 %collective-permute-start.16 = (bf16[3,256,128]{2,1,0:T(8,128)(2,1)S(1)}, bf16[3,256,128]{2,1,0:T(8,128)(2,1)S(1)}, u32[]{:S(2)}, u32[]{:S(2)}) collective-permute-start(bf16[3,256,128]{2,1,0:T(8,128)(2,1)S(1)} %add_convert_fusion.refs_1_), channel_id=1, source_target_pairs={{0,1},{1,0},{2,3},{3,2},{4,5},{5,4},{6,7},{7,6},{8,9},{9,8},{10,11... | collective-permute-start | bytes 589832 | tf_op jit(solution)/shard_map/ppermute | solution.py:532
  134.7 40.2 %collective-permute-start.21 = (bf16[2,3,256,512]{3,2,1,0:T(8,128)(2,1)}, bf16[2,3,256,512]{3,2,1,0:T(8,128)(2,1)}, u32[]{:S(2)}, u32[]{:S(2)}) collective-permute-start(bf16[2,3,256,512]{3,2,1,0:T(8,128)(2,1)} %get-tuple-element.46.refs_0_), channel_id=1, source_target_pairs={{0,24},{8,0},{17,9},{25,17},{2,26},{10,2},{19,11},{27,19},{4,28},{... | collective-permute-start | bytes 4718600 | tf_op jit(solution)/shard_map/ppermute | solution.py:588
  136.5 38.4 %collective-permute-start.20 = (bf16[2,3,256,512]{3,2,1,0:T(8,128)(2,1)}, bf16[2,3,256,512]{3,2,1,0:T(8,128)(2,1)}, u32[]{:S(2)}, u32[]{:S(2)}) collective-permute-start(bf16[2,3,256,512]{3,2,1,0:T(8,128)(2,1)} %get-tuple-element.46.refs_0_), channel_id=1, source_target_pairs={{0,8},{8,16},{17,25},{25,1},{2,10},{10,18},{19,27},{27,3},{4,12},{... | collective-permute-start | bytes 4718600 | tf_op jit(solution)/shard_map/ppermute | solution.py:588
  137.8 19.2 %collective-permute-start.22 = (bf16[2,3,256,128]{3,2,1,0:T(8,128)(2,1)S(1)}, bf16[2,3,256,128]{3,2,1,0:T(8,128)(2,1)S(1)}, u32[]{:S(2)}, u32[]{:S(2)}) collective-permute-start(bf16[2,3,256,128]{3,2,1,0:T(8,128)(2,1)S(1)} %get-tuple-element.47), channel_id=1, source_target_pairs={{1,16},{9,24},{16,1},{24,9},{3,18},{11,26},{18,3},{26,11},{5,20},{... | collective-permute-start | bytes 1179656 | tf_op jit(solution)/shard_map/ppermute | solution.py:587
  140.0 30.6 %all-to-all-start.3 = ((bf16[16,64,256]{2,1,0:T(8,128)(2,1)}), bf16[16,64,256]{2,1,0:T(8,128)(2,1)S(1)}, u32[]{:S(2)}, u32[]{:S(2)}) async-start(bf16[16,64,256]{2,1,0:T(8,128)(2,1)} %bitcast.16), calls=%async_computation.3 | async-start | bytes 1048576 | tf_op jit(solution)/shard_map/all_to_all | solution.py:589
  157.0 13.6 %collective-permute-start.25 = (bf16[2,3,256,128]{3,2,1,0:T(8,128)(2,1)S(1)}, bf16[2,3,256,128]{3,2,1,0:T(8,128)(2,1)S(1)}, u32[]{:S(2)}, u32[]{:S(2)}) collective-permute-start(bf16[2,3,256,128]{3,2,1,0:T(8,128)(2,1)S(1)} %collective-permute-done.22.refs_3_), channel_id=1, source_target_pairs={{1,33},{9,41},{16,48},{24,56},{33,65},{41,73},{48,80},{56,88},{65,... | collective-permute-start | bytes 1179656 | tf_op jit(solution)/shard_map/ppermute | solution.py:591
  159.9 13.1 %collective-permute-start.24 = (bf16[2,3,256,128]{3,2,1,0:T(8,128)(2,1)S(1)}, bf16[2,3,256,128]{3,2,1,0:T(8,128)(2,1)S(1)}, u32[]{:S(2)}, u32[]{:S(2)}) collective-permute-start(bf16[2,3,256,128]{3,2,1,0:T(8,128)(2,1)S(1)} %collective-permute-done.22.refs_3_), channel_id=1, source_target_pairs={{1,65},{9,73},{16,80},{24,88},{33,97},{41,105},{48,112},{56,120},{... | collective-permute-start | bytes 1179656 | tf_op jit(solution)/shard_map/ppermute | solution.py:591
  165.0 9.9 %collective-permute-start.23 = (bf16[2,3,256,128]{3,2,1,0:T(8,128)(2,1)S(1)}, bf16[2,3,256,128]{3,2,1,0:T(8,128)(2,1)S(1)}, u32[]{:S(2)}, u32[]{:S(2)}) collective-permute-start(bf16[2,3,256,128]{3,2,1,0:T(8,128)(2,1)S(1)} %collective-permute-done.22.refs_3_), channel_id=1, source_target_pairs={{1,97},{9,105},{16,112},{24,120},{33,1},{41,9},{48,16},{56,24},{65... | collective-permute-start | bytes 1179656 | tf_op jit(solution)/shard_map/ppermute | solution.py:591
  (16 other events, 88.8 us)
